TPU v7x, 128 devices: a whole 4x4x4 slice. The times are simulated.
128 devices in a mesh: lat: 32 (over z, x_hi, y), lon: 4 (over x_lo, core).
Axes of the slice: x: 4 (x_hi: 2, x_lo: 2; x = x_hi * 2 + x_lo), y: 4, z: 4, core: 2. Of those that a mesh axis runs over, the one named last changes fastest.
Arguments:
- height: float32 [4352, 9216], P('lat', 'lon'), may hold values from -6 to 6
- flux_east: float32 [4352, 9216], P('lat', 'lon'), may hold values from -4 to 4
- flux_north: float32 [4352, 9216], P('lat', 'lon'), may hold values from -4 to 4
- bathymetry: float32 [4352, 9216], P('lat', 'lon'), may hold values from -1 to 4
- wet_mask: int32 [4352, 9216], P('lat', 'lon'), may hold values 0 or 1
- wavenumber: int32 [32], replicated, may hold values from 0 to 4351, as said below
- legendre: bfloat16 [32, 4352, 4608], P('lat', None, 'lon'), may hold values from -0.0625 to 0.0625
- quadrature: float32 [4352], replicated, may hold values from 0.5 to 2
- love_factor: float32 [4608], P('lon'), may hold values from 0.2 to 1
Outputs:
- new_height: float32 [4352, 9216], P('lat', 'lon')
- new_east: float32 [4352, 9216], P('lat', 'lon')
- new_north: float32 [4352, 9216], P('lat', 'lon')
Inputs may be any that keep to these rules, and one draw needn't show every extreme that they name: `wavenumber`: the 32 values are distinct; 0 and 4351 are always among them.
All inputs are finite; a program needn't handle non-finite values. No bound on the sum of `wet_mask` on one device may be relied on, other than what follows from the above.
Results may differ from a plain program's by a relative error of at most 0.0003.
Values sent between devices are 32-bit elements; how exact they have to be, the bound alone decides.
No kernel may reach another device: no remote copies, remote signals or barrier semaphores. Data moves between devices by JAX's collectives and lax.ppermute only.
A program may use at most 128 MiB of HBM per device.

v0:
```python
import math

import jax
import jax.numpy as jnp
from jax import lax
from jax.sharding import PartitionSpec as P

STEPS = 12


gravity_step = 0.12
volume_step = 0.12
retain_factor = 0.97


def shifted(value, axis, steps):
    count = lax.axis_size(axis)
    pairs = [(source, (source + steps) % count) for source in range(count)]
    return lax.ppermute(value, axis, pairs)


def shifted_2(value, axis, by):
    length = lax.axis_size(axis)
    pairs = [(i, i + by) for i in range(length) if 0 <= i + by < length]
    return lax.ppermute(value, axis, pairs)


def shards(
    height,
    flux_east,
    flux_north,
    bathymetry,
    wet_mask,
    wavenumber,
    legendre,
    quadrature,
    love_factor,
):
    lon_count = lax.axis_size("lon")
    band_rows, block_cols = height.shape
    slot_total = wavenumber.shape[0]
    total_cols = block_cols * lon_count
    highest = lax.Precision.HIGHEST
    columns = lax.axis_index("lon") * block_cols + jnp.arange(block_cols, dtype=jnp.int32)
    product = wavenumber[:, None] * columns[None, :] % total_cols
    angle = product.astype(jnp.float32) * (2.0 * math.pi / total_cols)
    basis = jnp.concatenate([jnp.cos(angle), -jnp.sin(angle)], axis=0)
    wetness = wet_mask.astype(jnp.float32)
    analysis_scale = 1.0 / math.sqrt(total_cols)
    synthesis_scale = 1.0 / math.sqrt(total_cols)

    def advance(counter, carry):
        level, east, north = carry
        partial_value = (
            lax.dot_general(basis, level, (((1,), (1,)), ((), ())), precision=highest)
            * analysis_scale
        )
        partial_value = partial_value.reshape(2, slot_total, band_rows)
        summed = lax.psum(partial_value, "lon")
        spectral = lax.all_to_all(summed, "lat", split_axis=1, concat_axis=2, tiled=True)
        weighted = (spectral * quadrature).astype(jnp.bfloat16)
        coeff = jnp.einsum("ksr,srn->ksn", weighted, legendre, preferred_element_type=jnp.float32)
        scaled = (coeff * love_factor).astype(jnp.bfloat16)
        back_part = jnp.einsum("ksn,srn->ksr", scaled, legendre, preferred_element_type=jnp.float32)
        summed_back = lax.psum(back_part, "lon")
        bands = lax.all_to_all(summed_back, "lat", split_axis=2, concat_axis=1, tiled=True).reshape(
            2 * slot_total, band_rows
        )
        attraction = (
            lax.dot_general(bands, basis, (((0,), (0,)), ((), ())), precision=highest)
            * synthesis_scale
        )
        potential = level + attraction
        column_depth = wetness * jnp.maximum(bathymetry + level, 0.0)
        east_edge = jnp.stack([potential[:, 0], column_depth[:, 0], wetness[:, 0]])
        east_side = shifted(east_edge, "lon", -1)
        north_edge = jnp.stack([potential[0], column_depth[0], wetness[0]])
        north_side = shifted_2(north_edge, "lat", -1)
        potential_east = jnp.concatenate([potential[:, 1:], east_side[0][:, None]], axis=1)
        depth_east = jnp.concatenate([column_depth[:, 1:], east_side[1][:, None]], axis=1)
        wet_east = jnp.concatenate([wetness[:, 1:], east_side[2][:, None]], axis=1)
        potential_north = jnp.concatenate([potential[1:], north_side[0][None, :]], axis=0)
        depth_north = jnp.concatenate([column_depth[1:], north_side[1][None, :]], axis=0)
        wet_north = jnp.concatenate([wetness[1:], north_side[2][None, :]], axis=0)
        open_east = wetness * wet_east
        east_new = (
            retain_factor
            * open_east
            * (
                east
                - gravity_step
                * 0.5
                * (column_depth + depth_east)
                * open_east
                * (potential_east - potential)
            )
        )
        open_north = wetness * wet_north
        north_new = (
            retain_factor
            * open_north
            * (
                north
                - gravity_step
                * 0.5
                * (column_depth + depth_north)
                * open_north
                * (potential_north - potential)
            )
        )
        west_side = shifted(east_new[:, -1], "lon", 1)
        south_side = shifted_2(north_new[-1], "lat", 1)
        east_west = jnp.concatenate([west_side[:, None], east_new[:, :-1]], axis=1)
        north_south = jnp.concatenate([south_side[None, :], north_new[:-1]], axis=0)
        level_new = level - volume_step * wetness * (east_new - east_west + north_new - north_south)
        return (level_new, east_new, north_new)

    final = lax.fori_loop(0, STEPS, advance, (height, flux_east, flux_north))
    return (final[0], final[1], final[2])


def solution(mesh):
    placed = (
        P("lat", "lon"),
        P("lat", "lon"),
        P("lat", "lon"),
        P("lat", "lon"),
        P("lat", "lon"),
        P(),
        P("lat", None, "lon"),
        P(),
        P("lon"),
    )
    return jax.shard_map(
        shards,
        mesh=mesh,
        in_specs=placed,
        out_specs=(P("lat", "lon"), P("lat", "lon"), P("lat", "lon")),
        check_vma=False,
    )
```

profile of v0, /device:TPU:1, one launch (start us, length us, event | category | flops | bytes accessed | tf_op | source)
XLA Modules:
  0.0 1679.7 jit_solution(5727432963979431706)
XLA Ops:
  7.9 1670.8 %while.14 = (s32[]{:T(128)}, f32[136,2304]{1,0:T(8,128)S(1)}, f32[136,2304]{1,0:T(8,128)}, f32[136,2304]{1,0:T(8,128)}, f32[136,2304]{1,0:T(8,128)S(1)}, /*index...) while((s32[]{:T(128)}, f32[136,2304]{1,0:T(8,128)S(1)}, ...), condition=%wide.region_3.4_spmd, body=%wide.region_0.3_spmd.sunk | while | flops 533060928 | bytes 71701632 | solution.py:118
  68.6 22.4 %reduce.24 = f32[4352,2]{1,0:T(8,128)} reduce(f32[4352,1,2]{2,1,0:T(1,128)} %bitcast.105, f32[]{:T(128)} %broadcast.64), dimensions={1}, to_apply=%bitcast.54.reduce_sub_computation | reduce | bytes 69636 | tf_op jit(solution)/shard_map/while
  146.4 12.8 psum.16
  208.0 22.4 %reduce.24 = f32[4352,2]{1,0:T(8,128)} reduce(f32[4352,1,2]{2,1,0:T(1,128)} %bitcast.105, f32[]{:T(128)} %broadcast.64), dimensions={1}, to_apply=%bitcast.54.reduce_sub_computation | reduce | bytes 69636 | tf_op jit(solution)/shard_map/while
  285.9 12.8 psum.16
  347.4 22.4 %reduce.24 = f32[4352,2]{1,0:T(8,128)} reduce(f32[4352,1,2]{2,1,0:T(1,128)} %bitcast.105, f32[]{:T(128)} %broadcast.64), dimensions={1}, to_apply=%bitcast.54.reduce_sub_computation | reduce | bytes 69636 | tf_op jit(solution)/shard_map/while
  425.3 12.8 psum.16
  486.8 22.4 %reduce.24 = f32[4352,2]{1,0:T(8,128)} reduce(f32[4352,1,2]{2,1,0:T(1,128)} %bitcast.105, f32[]{:T(128)} %broadcast.64), dimensions={1}, to_apply=%bitcast.54.reduce_sub_computation | reduce | bytes 69636 | tf_op jit(solution)/shard_map/while
  564.7 12.8 psum.16
  626.3 22.4 %reduce.24 = f32[4352,2]{1,0:T(8,128)} reduce(f32[4352,1,2]{2,1,0:T(1,128)} %bitcast.105, f32[]{:T(128)} %broadcast.64), dimensions={1}, to_apply=%bitcast.54.reduce_sub_computation | reduce | bytes 69636 | tf_op jit(solution)/shard_map/while
  704.1 12.8 psum.16
  765.7 22.4 %reduce.24 = f32[4352,2]{1,0:T(8,128)} reduce(f32[4352,1,2]{2,1,0:T(1,128)} %bitcast.105, f32[]{:T(128)} %broadcast.64), dimensions={1}, to_apply=%bitcast.54.reduce_sub_computation | reduce | bytes 69636 | tf_op jit(solution)/shard_map/while
  843.6 12.8 psum.16
  905.1 22.4 %reduce.24 = f32[4352,2]{1,0:T(8,128)} reduce(f32[4352,1,2]{2,1,0:T(1,128)} %bitcast.105, f32[]{:T(128)} %broadcast.64), dimensions={1}, to_apply=%bitcast.54.reduce_sub_computation | reduce | bytes 69636 | tf_op jit(solution)/shard_map/while
  983.0 12.8 psum.16
  1044.5 22.4 %reduce.24 = f32[4352,2]{1,0:T(8,128)} reduce(f32[4352,1,2]{2,1,0:T(1,128)} %bitcast.105, f32[]{:T(128)} %broadcast.64), dimensions={1}, to_apply=%bitcast.54.reduce_sub_computation | reduce | bytes 69636 | tf_op jit(solution)/shard_map/while
  1122.4 12.8 psum.16
  1184.0 22.4 %reduce.24 = f32[4352,2]{1,0:T(8,128)} reduce(f32[4352,1,2]{2,1,0:T(1,128)} %bitcast.105, f32[]{:T(128)} %broadcast.64), dimensions={1}, to_apply=%bitcast.54.reduce_sub_computation | reduce | bytes 69636 | tf_op jit(solution)/shard_map/while
  1261.8 12.8 psum.16
  1323.4 22.4 %reduce.24 = f32[4352,2]{1,0:T(8,128)} reduce(f32[4352,1,2]{2,1,0:T(1,128)} %bitcast.105, f32[]{:T(128)} %broadcast.64), dimensions={1}, to_apply=%bitcast.54.reduce_sub_computation | reduce | bytes 69636 | tf_op jit(solution)/shard_map/while
  1401.3 12.8 psum.16
  1462.8 22.4 %reduce.24 = f32[4352,2]{1,0:T(8,128)} reduce(f32[4352,1,2]{2,1,0:T(1,128)} %bitcast.105, f32[]{:T(128)} %broadcast.64), dimensions={1}, to_apply=%bitcast.54.reduce_sub_computation | reduce | bytes 69636 | tf_op jit(solution)/shard_map/while
  1540.7 12.8 psum.16
  1602.2 22.4 %reduce.24 = f32[4352,2]{1,0:T(8,128)} reduce(f32[4352,1,2]{2,1,0:T(1,128)} %bitcast.105, f32[]{:T(128)} %broadcast.64), dimensions={1}, to_apply=%bitcast.54.reduce_sub_computation | reduce | bytes 69636 | tf_op jit(solution)/shard_map/while
  (727 shorter events, 1266.8 us)
Async XLA Ops:
  21.5 19.6 %all-to-all-start = ((f32[2,32,136]{2,0,1:T(2,128)}), f32[2,32,136]{2,0,1:T(2,128)S(1)}, u32[]{:S(2)}, u32[]{:S(2)}) async-start(f32[2,32,136]{2,0,1:T(2,128)} %psum.16), calls=%async_computation | async-start | bytes 131072 | tf_op jit(solution)/shard_map/while/body/eval_jaxpr/all_to_all | solution.py:60
  94.5 12.6 all-to-all-start.1
  159.2 21.4 %all-to-all-start = ((f32[2,32,136]{2,0,1:T(2,128)}), f32[2,32,136]{2,0,1:T(2,128)S(1)}, u32[]{:S(2)}, u32[]{:S(2)}) async-start(f32[2,32,136]{2,0,1:T(2,128)} %psum.16), calls=%async_computation | async-start | bytes 131072 | tf_op jit(solution)/shard_map/while/body/eval_jaxpr/all_to_all | solution.py:60
  233.9 12.6 all-to-all-start.1
  298.6 21.3 %all-to-all-start = ((f32[2,32,136]{2,0,1:T(2,128)}), f32[2,32,136]{2,0,1:T(2,128)S(1)}, u32[]{:S(2)}, u32[]{:S(2)}) async-start(f32[2,32,136]{2,0,1:T(2,128)} %psum.16), calls=%async_computation | async-start | bytes 131072 | tf_op jit(solution)/shard_map/while/body/eval_jaxpr/all_to_all | solution.py:60
  373.3 12.6 all-to-all-start.1
  438.1 21.4 %all-to-all-start = ((f32[2,32,136]{2,0,1:T(2,128)}), f32[2,32,136]{2,0,1:T(2,128)S(1)}, u32[]{:S(2)}, u32[]{:S(2)}) async-start(f32[2,32,136]{2,0,1:T(2,128)} %psum.16), calls=%async_computation | async-start | bytes 131072 | tf_op jit(solution)/shard_map/while/body/eval_jaxpr/all_to_all | solution.py:60
  512.8 12.6 all-to-all-start.1
  577.5 21.3 %all-to-all-start = ((f32[2,32,136]{2,0,1:T(2,128)}), f32[2,32,136]{2,0,1:T(2,128)S(1)}, u32[]{:S(2)}, u32[]{:S(2)}) async-start(f32[2,32,136]{2,0,1:T(2,128)} %psum.16), calls=%async_computation | async-start | bytes 131072 | tf_op jit(solution)/shard_map/while/body/eval_jaxpr/all_to_all | solution.py:60
  652.2 12.6 all-to-all-start.1
  716.9 21.4 %all-to-all-start = ((f32[2,32,136]{2,0,1:T(2,128)}), f32[2,32,136]{2,0,1:T(2,128)S(1)}, u32[]{:S(2)}, u32[]{:S(2)}) async-start(f32[2,32,136]{2,0,1:T(2,128)} %psum.16), calls=%async_computation | async-start | bytes 131072 | tf_op jit(solution)/shard_map/while/body/eval_jaxpr/all_to_all | solution.py:60
  791.6 12.6 all-to-all-start.1
  856.3 21.3 %all-to-all-start = ((f32[2,32,136]{2,0,1:T(2,128)}), f32[2,32,136]{2,0,1:T(2,128)S(1)}, u32[]{:S(2)}, u32[]{:S(2)}) async-start(f32[2,32,136]{2,0,1:T(2,128)} %psum.16), calls=%async_computation | async-start | bytes 131072 | tf_op jit(solution)/shard_map/while/body/eval_jaxpr/all_to_all | solution.py:60
  931.0 12.6 all-to-all-start.1
  995.8 21.4 %all-to-all-start = ((f32[2,32,136]{2,0,1:T(2,128)}), f32[2,32,136]{2,0,1:T(2,128)S(1)}, u32[]{:S(2)}, u32[]{:S(2)}) async-start(f32[2,32,136]{2,0,1:T(2,128)} %psum.16), calls=%async_computation | async-start | bytes 131072 | tf_op jit(solution)/shard_map/while/body/eval_jaxpr/all_to_all | solution.py:60
  1070.5 12.6 all-to-all-start.1
  1135.2 21.3 %all-to-all-start = ((f32[2,32,136]{2,0,1:T(2,128)}), f32[2,32,136]{2,0,1:T(2,128)S(1)}, u32[]{:S(2)}, u32[]{:S(2)}) async-start(f32[2,32,136]{2,0,1:T(2,128)} %psum.16), calls=%async_computation | async-start | bytes 131072 | tf_op jit(solution)/shard_map/while/body/eval_jaxpr/all_to_all | solution.py:60
  1209.9 12.6 all-to-all-start.1
  1274.6 21.4 %all-to-all-start = ((f32[2,32,136]{2,0,1:T(2,128)}), f32[2,32,136]{2,0,1:T(2,128)S(1)}, u32[]{:S(2)}, u32[]{:S(2)}) async-start(f32[2,32,136]{2,0,1:T(2,128)} %psum.16), calls=%async_computation | async-start | bytes 131072 | tf_op jit(solution)/shard_map/while/body/eval_jaxpr/all_to_all | solution.py:60
  1349.3 12.6 all-to-all-start.1
  1414.0 21.3 %all-to-all-start = ((f32[2,32,136]{2,0,1:T(2,128)}), f32[2,32,136]{2,0,1:T(2,128)S(1)}, u32[]{:S(2)}, u32[]{:S(2)}) async-start(f32[2,32,136]{2,0,1:T(2,128)} %psum.16), calls=%async_computation | async-start | bytes 131072 | tf_op jit(solution)/shard_map/while/body/eval_jaxpr/all_to_all | solution.py:60
  1488.7 12.6 all-to-all-start.1
  1553.5 21.4 %all-to-all-start = ((f32[2,32,136]{2,0,1:T(2,128)}), f32[2,32,136]{2,0,1:T(2,128)S(1)}, u32[]{:S(2)}, u32[]{:S(2)}) async-start(f32[2,32,136]{2,0,1:T(2,128)} %psum.16), calls=%async_computation | async-start | bytes 131072 | tf_op jit(solution)/shard_map/while/body/eval_jaxpr/all_to_all | solution.py:60
  1628.2 12.6 all-to-all-start.1
  (90 other events, 346.4 us)
where the time goes:
time: 1690 us; the launch traced here: 1680 us
  other arithmetic  431 us (26%)
  local copies, waits for them, and re-layouts  374 us (22%)
  blocking collectives  301 us (18%)
  starting transfers between devices  277 us (16%)
  matrix products  160 us (9%)
  waiting for transfers between devices  134 us (8%)
    while x12, other arithmetic  269 us
    psum x12, blocking collectives, advance(): summed = lax.psum(partial_value, 'lon')  153 us
    all_to_all x12, starting transfers between devices, advance(): lax.all_to_all(summed, 'lat', split_axis=1, concat_axis=2, tiled=True)  148 us
    psum x12, blocking collectives, advance(): summed_back = lax.psum(back_part, 'lon')  148 us
    dot_general x12, matrix products, advance(): jnp.einsum('ksn,srn->ksr', scaled, legendre, preferred_element_type=jnp.f...  128 us
    while x84, local copies, waits for them, and re-layouts  105 us
    mul x12, other arithmetic, advance(): retain_factor * open_east  78.2 us
    all_to_all x12, waiting for transfers between devices, advance(): lax.all_to_all(summed, 'lat', split_axis=1, concat_axis=2, tiled=True)  72 us
  transfers between devices with their start and end apart: 72, of which 48 were waited for; matrix products, arithmetic and copies ran while one was open for 10% of the time, Pallas kernels for 0%

commit v1 on v0

v1 whole, which is shorter than its diff:
```python
import math

import jax
import jax.numpy as jnp
from jax import lax
from jax.experimental import pallas as pl
from jax.experimental.pallas import tpu as pltpu
from jax.sharding import PartitionSpec as P

STEPS = 12
HALO = STEPS
LANES = 128
MSG = 256

gravity_step = 0.12
volume_step = 0.12
retain_factor = 0.97

BOTH = ("lat", "lon")
VMEM = pl.BlockSpec(memory_space=pltpu.VMEM)
HIGH = jnp.float32
LOW = jnp.bfloat16


def in_vmem(value):
    return pltpu.with_memory_space_constraint(value, pltpu.VMEM)


def split_pair(value):
    high = value.astype(LOW)
    return high, (value - high.astype(HIGH)).astype(LOW)


def fourier_sums(rows, level_ref, table_ref, out_ref):
    cols = table_ref.shape[0]
    total = jnp.zeros((2 * rows, LANES), HIGH)
    for start in range(0, cols, 256):
        high, low = split_pair(level_ref[:rows, start : start + 256])
        both = jnp.concatenate([high, low], axis=0)
        total = total + jnp.dot(both, table_ref[start : start + 256, :], preferred_element_type=HIGH)
    half = total[:rows] + total[rows:]
    half = half + pltpu.roll(half, LANES // 2, 1)
    half = jnp.concatenate([half, jnp.zeros((MSG - rows, LANES), HIGH)], axis=0)
    sums = jnp.transpose(half)
    slots = out_ref.shape[0] // 4
    for slot in range(slots):
        pair = sums[2 * slot : 2 * slot + 2, :]
        for part in range(4):
            out_ref[4 * slot + part] = pair


def first_kernel(rows, level_ref, table_ref, out_ref):
    fourier_sums(rows, level_ref, table_ref, out_ref)


def grid_kernel(
    rows,
    got_ref,
    level_in,
    east_in,
    north_in,
    bathy_ref,
    wet_ref,
    east_open_ref,
    north_open_ref,
    synth_ref,
    table_ref,
    level_ref,
    east_ref,
    north_ref,
    out_ref,
    back_ref,
    pot_ref,
    depth_ref,
):
    tall, wide = level_in.shape
    slots = got_ref.shape[0] // 4
    for slot in range(slots):
        pair = got_ref[4 * slot]
        for part in range(1, 4):
            pair = pair + got_ref[4 * slot + part]
        back_ref[2 * slot : 2 * slot + 2, :] = pair
    back = back_ref[...] * (1.0 / math.sqrt(4 * table_ref.shape[0]))
    lane = lax.broadcasted_iota(jnp.int32, back.shape, 1)
    back = jnp.where(
        lane < tall - HALO, pltpu.roll(back, MSG - HALO, 1), pltpu.roll(back, tall - HALO, 1)
    )
    high, low = split_pair(back)
    high, low = high.astype(HIGH), low.astype(HIGH)
    stacked = jnp.concatenate([high, high, low, jnp.zeros_like(low)], axis=0)
    factors = jnp.transpose(stacked)[:tall].astype(LOW)
    half_gravity = gravity_step * 0.5
    for start in range(0, wide, 256):
        block = slice(start, min(start + 256, wide))
        pull = jnp.dot(factors, synth_ref[:, block], preferred_element_type=HIGH)
        level = level_in[:, block]
        pot_ref[:tall, block] = level + pull
        depth_ref[:tall, block] = (half_gravity * wet_ref[:, block]) * jnp.maximum(
            bathy_ref[:, block] + level, 0.0
        )
    pot_ref[tall:, :] = pot_ref[:8, :]
    depth_ref[tall:, :] = depth_ref[:8, :]

    def fluxes(start):
        here = slice(start, start + 8)
        above = slice(start + 1, start + 9)
        pot, depth = pot_ref[here, :], depth_ref[here, :]
        pot_east, depth_east = pltpu.roll(pot, wide - 1, 1), pltpu.roll(depth, wide - 1, 1)
        east_ref[here, :] = east_open_ref[here, :] * (
            east_in[here, :] - (depth + depth_east) * (pot_east - pot)
        )
        north_ref[here, :] = north_open_ref[here, :] * (
            north_in[here, :] - (depth + depth_ref[above, :]) * (pot_ref[above, :] - pot)
        )

    def levels(start):
        here = slice(start, start + 8)
        east, north = east_ref[here, :], north_ref[here, :]
        if start:
            below = north_ref[start - 1 : start + 7, :]
        else:
            below = jnp.concatenate([north_ref[tall - 1 :, :], north_ref[:7, :]], axis=0)
        level_ref[here, :] = level_in[here, :] - (volume_step * wet_ref[here, :]) * (
            east - pltpu.roll(east, 1, 1) + north - below
        )

    for start in range(0, tall, 8):
        fluxes(start)
        if start:
            levels(start)
    levels(0)
    fourier_sums(rows, level_ref, table_ref, out_ref)


def legendre_kernel(band, got_ref, legendre_ref, weight_ref, love_ref, out_ref, line_ref, back_ref):
    total, degrees = legendre_ref.shape
    bands = total // band
    line_ref[...] = jnp.zeros_like(line_ref)
    lane = lax.broadcasted_iota(jnp.int32, (8, MSG), 1)
    for index in range(bands):
        pair = got_ref[4 * index]
        for part in range(1, 4):
            pair = pair + got_ref[4 * index + part]
        piece = jnp.concatenate([pair, jnp.zeros((6, MSG), HIGH)], axis=0)
        piece = jnp.where(lane < band, piece, 0.0)
        tile, offset = divmod(band * index, LANES)
        if offset:
            piece = pltpu.roll(piece, offset, 1)
        where = slice(tile * LANES, tile * LANES + MSG)
        line_ref[:, where] = line_ref[:, where] + piece
    coeff = jnp.zeros((8, degrees), HIGH)
    for start in range(0, total, 256):
        where = slice(start, start + 256)
        weighted = (line_ref[:, where] * weight_ref[:, where]).astype(LOW)
        coeff = coeff + jnp.dot(weighted, legendre_ref[where, :], preferred_element_type=HIGH)
    scaled = (coeff * love_ref[...]).astype(LOW)
    back_ref[:, :LANES] = jnp.zeros((8, LANES), HIGH)
    back_ref[:, LANES + total :] = jnp.zeros((8, back_ref.shape[1] - LANES - total), HIGH)
    for start in range(0, total, 256):
        back_ref[:, LANES + start : LANES + start + 256] = lax.dot_general(
            scaled,
            legendre_ref[start : start + 256, :],
            (((1,), (1,)), ((), ())),
            preferred_element_type=HIGH,
        )
    for index in range(bands):
        tile, offset = divmod(band * index - HALO + LANES, LANES)
        piece = back_ref[:, tile * LANES : tile * LANES + 384]
        if offset:
            piece = pltpu.roll(piece, 384 - offset, 1)
        pair = piece[:2, :MSG]
        for part in range(4):
            out_ref[4 * index + part] = pair


def shifted(value, axis, by):
    count = lax.axis_size(axis)
    return lax.ppermute(value, axis, [(i, (i + by) % count) for i in range(count)])


def shifted_open(value, axis, by):
    count = lax.axis_size(axis)
    pairs = [(i, i + by) for i in range(count) if 0 <= i + by < count]
    return lax.ppermute(value, axis, pairs)


def with_ghosts(fields):
    rows = fields[0].shape[0]
    from_east = shifted(jnp.stack([f[:, :LANES] for f in fields]), "lon", -1)
    from_west = shifted(jnp.stack([f[:, -LANES:] for f in fields]), "lon", 1)
    lane = lax.broadcasted_iota(jnp.int32, from_east.shape, 2)
    tile = jnp.where(lane < HALO, from_east, jnp.where(lane >= LANES - HALO, from_west, 0.0))
    wide = [jnp.concatenate([f, tile[i]], axis=1) for i, f in enumerate(fields)]
    from_north = shifted_open(jnp.stack([f[:16] for f in wide]), "lat", -1)
    from_south = shifted_open(jnp.stack([f[rows - 16 :] for f in wide]), "lat", 1)
    return [
        jnp.concatenate([f, from_north[i, :HALO], from_south[i, 16 - HALO :]], axis=0)
        for i, f in enumerate(wide)
    ]


def shards(
    height,
    flux_east,
    flux_north,
    bathymetry,
    wet_mask,
    wavenumber,
    legendre,
    quadrature,
    love_factor,
):
    lon_count = lax.axis_size("lon")
    lat_count = lax.axis_size("lat")
    rows, cols = height.shape
    slots = wavenumber.shape[0]
    total_cols = cols * lon_count
    total_rows = rows * lat_count
    tall, wide = rows + 2 * HALO, cols + LANES
    devices = lat_count * lon_count
    padded_rows = -(-rows // 16) * 16

    lane = jnp.arange(wide, dtype=jnp.int32)
    offset = jnp.where(lane < cols + LANES // 2, lane, lane - wide)
    columns = (lax.axis_index("lon") * cols + offset + total_cols) % total_cols
    product = wavenumber[:, None] * columns[None, :] % total_cols
    angle = product.astype(HIGH) * (2.0 * math.pi / total_cols)
    basis = jnp.stack([jnp.cos(angle), -jnp.sin(angle)], axis=1).reshape(2 * slots, wide)
    basis_high = lax.reduce_precision(basis, 8, 7)
    basis_low = (basis - basis_high).astype(LOW)
    basis_high = basis_high.astype(LOW)
    synth = jnp.concatenate([basis_high, basis_low, basis_high, jnp.zeros_like(basis_low)], axis=0)
    table = jnp.concatenate([basis_high[:, :cols], basis_low[:, :cols]], axis=0).T

    wetness = wet_mask.astype(HIGH)
    level, east, north, bathy, wet = with_ghosts(
        [height, flux_east, flux_north, bathymetry, wetness]
    )
    row = lax.broadcasted_iota(jnp.int32, (tall, wide), 0)
    east_open = retain_factor * wet * jnp.roll(wet, -1, axis=1)
    north_open = retain_factor * wet * jnp.roll(wet, -1, axis=0)
    north_open = jnp.where(row == rows + HALO - 1, 0.0, north_open)
    weight = jnp.broadcast_to((quadrature / math.sqrt(total_cols))[None, :], (8, total_rows))
    love = jnp.broadcast_to(love_factor[None, :], (8, love_factor.shape[0]))
    legendre = legendre.reshape(legendre.shape[1:])

    field = jax.ShapeDtypeStruct((tall, wide), HIGH)
    message = jax.ShapeDtypeStruct((devices, 2, MSG), HIGH)
    small = pltpu.CompilerParams(vmem_limit_bytes=24 * 2**20)

    sums = pl.pallas_call(
        lambda *refs: first_kernel(padded_rows, *refs),
        out_shape=message,
        in_specs=[VMEM] * 2,
        out_specs=VMEM,
        compiler_params=small,
        name="first_sums",
    )(in_vmem(level), in_vmem(table))

    def advance(counter, carry):
        level, east, north, sums = carry
        spectral = lax.all_to_all(sums, BOTH, split_axis=0, concat_axis=0, tiled=True)
        back = pl.pallas_call(
            lambda *refs: legendre_kernel(rows, *refs),
            out_shape=message,
            in_specs=[VMEM] * 4,
            out_specs=VMEM,
            scratch_shapes=[
                pltpu.VMEM((8, total_rows + LANES), HIGH),
                pltpu.VMEM((8, total_rows + 4 * LANES), HIGH),
            ],
            compiler_params=small,
            name="legendre_pair",
        )(spectral, in_vmem(legendre), in_vmem(weight), in_vmem(love))
        bands = lax.all_to_all(back, BOTH, split_axis=0, concat_axis=0, tiled=True)
        return pl.pallas_call(
            lambda *refs: grid_kernel(padded_rows, *refs),
            out_shape=(field, field, field, message),
            in_specs=[VMEM] * 10,
            out_specs=(VMEM,) * 4,
            scratch_shapes=[
                pltpu.VMEM((2 * slots, MSG), HIGH),
                pltpu.VMEM((tall + 8, wide), HIGH),
                pltpu.VMEM((tall + 8, wide), HIGH),
            ],
            input_output_aliases={1: 0, 2: 1, 3: 2},
            compiler_params=small,
            name="grid_update",
        )(
            bands,
            in_vmem(level),
            in_vmem(east),
            in_vmem(north),
            in_vmem(bathy),
            in_vmem(wet),
            in_vmem(east_open),
            in_vmem(north_open),
            in_vmem(synth),
            in_vmem(table),
        )

    carry = (level, east, north, sums)
    for counter in range(STEPS):
        carry = advance(counter, carry)
    level, east, north, sums = carry
    return (level[:rows, :cols], east[:rows, :cols], north[:rows, :cols])


def solution(mesh):
    placed = (
        P("lat", "lon"),
        P("lat", "lon"),
        P("lat", "lon"),
        P("lat", "lon"),
        P("lat", "lon"),
        P(),
        P("lat", None, "lon"),
        P(),
        P("lon"),
    )
    return jax.shard_map(
        shards,
        mesh=mesh,
        in_specs=placed,
        out_specs=(P("lat", "lon"), P("lat", "lon"), P("lat", "lon")),
        check_vma=False,
    )
```

time: 1690 us -> 565 us (0.33)
  other arithmetic: 431 us -> 22.4 us
  local copies, waits for them, and re-layouts: 374 us -> 44.1 us
  starting transfers between devices: 277 us -> 30.6 us
  matrix products: 160 us -> 0 us
  waiting for transfers between devices: 134 us -> 28.1 us
  Pallas kernels: 0 us -> 93.9 us
  blocking collectives: 301 us -> 337 us
    all_to_all x0 -> x22, blocking collectives: none -> 337 us  [the longest x11 168 us: advance(): bands = lax.all_to_all(back, BOTH, split_axis=0, concat_axis=0, tiled=True)]
    psum x24 -> x0, blocking collectives: 301 us -> none  [the longest x12 153 us: advance(): summed = lax.psum(partial_value, 'lon')]
    while x12 -> x0, other arithmetic: 269 us -> none
    all_to_all x24 -> x2, starting transfers between devices: 195 us -> 22.7 us  [the longest x1 16.5 us: advance(): lax.all_to_all(sums, BOTH, split_axis=0, concat_axis=0, tiled=True)]
    dot_general x36 -> x0, matrix products: 160 us -> none  [the longest x12 128 us: advance(): jnp.einsum('ksn,srn->ksr', scaled, legendre, preferred_element_type=jnp.f...]
    slice x192 -> x9, local copies, waits for them, and re-layouts: 150 us -> 7.34 us  [the longest x3 3.35 us: shards(): return (level[:rows, :cols], east[:rows, :cols], north[:rows, :cols])]
    mul x24 -> x0, other arithmetic: 110 us -> none  [the longest x12 78.2 us: advance(): retain_factor * open_east]
    while x84 -> x0, local copies, waits for them, and re-layouts: 105 us -> none
  transfers between devices with their start and end apart: 72 -> 6, of which waited for: 48 -> 6; matrix products, arithmetic and copies ran while one was open for 10% -> 4% of each run, Pallas kernels for 0% -> 0%
where the time goes in v1:
time: 565 us; the launch traced here: 558 us
  blocking collectives  337 us (60%)
  Pallas kernels  93.9 us (17%)
  local copies, waits for them, and re-layouts  44.1 us (8%)
  starting transfers between devices  30.6 us (5%)
  waiting for transfers between devices  28.1 us (5%)
  other arithmetic  22.4 us (4%)
    all_to_all x11, blocking collectives, advance(): bands = lax.all_to_all(back, BOTH, split_axis=0, concat_axis=0, tiled=True)  168 us
    all_to_all x11, blocking collectives, advance(): lax.all_to_all(sums, BOTH, split_axis=0, concat_axis=0, tiled=True)  168 us
    pallas_call x12, Pallas kernels, advance(): pl.pallas_call(lambda *refs: legendre_kernel(rows, *refs), out_shape=mess...  50.6 us
    pallas_call x12, Pallas kernels, advance(): pl.pallas_call(lambda *refs: grid_kernel(padded_rows, *refs), out_shape=(...  41.9 us
    unnamed x104, local copies, waits for them, and re-layouts  27.8 us
    all_to_all x1, starting transfers between devices, advance(): lax.all_to_all(sums, BOTH, split_axis=0, concat_axis=0, tiled=True)  16.5 us
    ppermute x2, waiting for transfers between devices, shifted_open(): return lax.ppermute(value, axis, pairs)  14.6 us
  transfers between devices with their start and end apart: 6, of which 6 were waited for; matrix products, arithmetic and copies ran while one was open for 4% of the time, Pallas kernels for 0%

profile of v1, /device:TPU:1, one launch (start us, length us, event | category | flops | bytes accessed | tf_op | source)
XLA Modules:
  0.0 557.7 jit_solution(14124680324402671648)
XLA Ops:
  35.7 11.2 %collective-permute-done.2 = f32[5,16,2432]{2,1,0:T(8,128)} collective-permute-done((f32[5,16,2432]{2,1,0:T(8,128)}, f32[5,16,2432]{2,1,0:T(8,128)}, u32[]{:S(2)}, u32[]{:S(2)}) %collective-permute-start.2) | collective-permute-done | bytes 778272 | tf_op jit(solution)/shard_map/ppermute | solution.py:184
  58.1 16.5 %all-to-all-start = ((f32[128,2,256]{2,1,0:T(2,128)}), f32[128,2,256]{2,1,0:T(2,128)S(1)}, u32[]{:S(2)}, u32[]{:S(2)}) async-start(f32[128,2,256]{2,1,0:T(2,128)} %first_sums.1), calls=%async_computation | async-start | bytes 524288 | tf_op jit(solution)/shard_map/all_to_all | solution.py:262
  127.4 15.2 %all_to_all.120.refs_0_ = f32[128,2,256]{2,1,0:T(2,128)S(1)} all-to-all(f32[128,2,256]{2,1,0:T(2,128)S(1)} %get-tuple-element.50), channel_id=1, replica_groups=mesh['lat'=32,'lon'=4] {'lat','lon'}, dimensions={0} | all-to-all | bytes 524288 | tf_op jit(solution)/shard_map/all_to_all | solution.py:262
  150.7 15.6 %all_to_all.121.refs_0_ = f32[128,2,256]{2,1,0:T(2,128)S(1)} all-to-all(f32[128,2,256]{2,1,0:T(2,128)S(1)} %legendre_pair.13), channel_id=1, replica_groups=mesh['lat'=32,'lon'=4] {'lat','lon'}, dimensions={0} | all-to-all | bytes 524288 | tf_op jit(solution)/shard_map/all_to_all | solution.py:275
  171.2 15.2 %all_to_all.122.refs_0_ = f32[128,2,256]{2,1,0:T(2,128)S(1)} all-to-all(f32[128,2,256]{2,1,0:T(2,128)S(1)} %get-tuple-element.54), channel_id=1, replica_groups=mesh['lat'=32,'lon'=4] {'lat','lon'}, dimensions={0} | all-to-all | bytes 524288 | tf_op jit(solution)/shard_map/all_to_all | solution.py:262
  190.6 15.2 %all_to_all.123.refs_0_ = f32[128,2,256]{2,1,0:T(2,128)S(1)} all-to-all(f32[128,2,256]{2,1,0:T(2,128)S(1)} %legendre_pair.14), channel_id=1, replica_groups=mesh['lat'=32,'lon'=4] {'lat','lon'}, dimensions={0} | all-to-all | bytes 524288 | tf_op jit(solution)/shard_map/all_to_all | solution.py:275
  209.3 15.4 %all_to_all.124.refs_0_ = f32[128,2,256]{2,1,0:T(2,128)S(1)} all-to-all(f32[128,2,256]{2,1,0:T(2,128)S(1)} %get-tuple-element.58), channel_id=1, replica_groups=mesh['lat'=32,'lon'=4] {'lat','lon'}, dimensions={0} | all-to-all | bytes 524288 | tf_op jit(solution)/shard_map/all_to_all | solution.py:262
  228.9 15.2 %all_to_all.125.refs_0_ = f32[128,2,256]{2,1,0:T(2,128)S(1)} all-to-all(f32[128,2,256]{2,1,0:T(2,128)S(1)} %legendre_pair.15), channel_id=1, replica_groups=mesh['lat'=32,'lon'=4] {'lat','lon'}, dimensions={0} | all-to-all | bytes 524288 | tf_op jit(solution)/shard_map/all_to_all | solution.py:275
  247.5 15.2 %all_to_all.126.refs_0_ = f32[128,2,256]{2,1,0:T(2,128)S(1)} all-to-all(f32[128,2,256]{2,1,0:T(2,128)S(1)} %get-tuple-element.62), channel_id=1, replica_groups=mesh['lat'=32,'lon'=4] {'lat','lon'}, dimensions={0} | all-to-all | bytes 524288 | tf_op jit(solution)/shard_map/all_to_all | solution.py:262
  266.9 15.4 %all_to_all.127.refs_0_ = f32[128,2,256]{2,1,0:T(2,128)S(1)} all-to-all(f32[128,2,256]{2,1,0:T(2,128)S(1)} %legendre_pair.16), channel_id=1, replica_groups=mesh['lat'=32,'lon'=4] {'lat','lon'}, dimensions={0} | all-to-all | bytes 524288 | tf_op jit(solution)/shard_map/all_to_all | solution.py:275
  285.8 15.2 %all_to_all.128.refs_0_ = f32[128,2,256]{2,1,0:T(2,128)S(1)} all-to-all(f32[128,2,256]{2,1,0:T(2,128)S(1)} %get-tuple-element.66), channel_id=1, replica_groups=mesh['lat'=32,'lon'=4] {'lat','lon'}, dimensions={0} | all-to-all | bytes 524288 | tf_op jit(solution)/shard_map/all_to_all | solution.py:262
  305.2 15.2 %all_to_all.129.refs_0_ = f32[128,2,256]{2,1,0:T(2,128)S(1)} all-to-all(f32[128,2,256]{2,1,0:T(2,128)S(1)} %legendre_pair.17), channel_id=1, replica_groups=mesh['lat'=32,'lon'=4] {'lat','lon'}, dimensions={0} | all-to-all | bytes 524288 | tf_op jit(solution)/shard_map/all_to_all | solution.py:275
  323.9 15.6 %all_to_all.130.refs_0_ = f32[128,2,256]{2,1,0:T(2,128)S(1)} all-to-all(f32[128,2,256]{2,1,0:T(2,128)S(1)} %get-tuple-element.70), channel_id=1, replica_groups=mesh['lat'=32,'lon'=4] {'lat','lon'}, dimensions={0} | all-to-all | bytes 524288 | tf_op jit(solution)/shard_map/all_to_all | solution.py:262
  343.7 15.2 %all_to_all.131.refs_0_ = f32[128,2,256]{2,1,0:T(2,128)S(1)} all-to-all(f32[128,2,256]{2,1,0:T(2,128)S(1)} %legendre_pair.18), channel_id=1, replica_groups=mesh['lat'=32,'lon'=4] {'lat','lon'}, dimensions={0} | all-to-all | bytes 524288 | tf_op jit(solution)/shard_map/all_to_all | solution.py:275
  362.3 15.2 %all_to_all.132.refs_0_ = f32[128,2,256]{2,1,0:T(2,128)S(1)} all-to-all(f32[128,2,256]{2,1,0:T(2,128)S(1)} %get-tuple-element.74), channel_id=1, replica_groups=mesh['lat'=32,'lon'=4] {'lat','lon'}, dimensions={0} | all-to-all | bytes 524288 | tf_op jit(solution)/shard_map/all_to_all | solution.py:262
  381.7 15.4 %all_to_all.133.refs_0_ = f32[128,2,256]{2,1,0:T(2,128)S(1)} all-to-all(f32[128,2,256]{2,1,0:T(2,128)S(1)} %legendre_pair.19), channel_id=1, replica_groups=mesh['lat'=32,'lon'=4] {'lat','lon'}, dimensions={0} | all-to-all | bytes 524288 | tf_op jit(solution)/shard_map/all_to_all | solution.py:275
  400.6 15.2 %all_to_all.134.refs_0_ = f32[128,2,256]{2,1,0:T(2,128)S(1)} all-to-all(f32[128,2,256]{2,1,0:T(2,128)S(1)} %get-tuple-element.78), channel_id=1, replica_groups=mesh['lat'=32,'lon'=4] {'lat','lon'}, dimensions={0} | all-to-all | bytes 524288 | tf_op jit(solution)/shard_map/all_to_all | solution.py:262
  420.0 15.2 %all_to_all.135.refs_0_ = f32[128,2,256]{2,1,0:T(2,128)S(1)} all-to-all(f32[128,2,256]{2,1,0:T(2,128)S(1)} %legendre_pair.20), channel_id=1, replica_groups=mesh['lat'=32,'lon'=4] {'lat','lon'}, dimensions={0} | all-to-all | bytes 524288 | tf_op jit(solution)/shard_map/all_to_all | solution.py:275
  438.6 15.4 %all_to_all.136.refs_0_ = f32[128,2,256]{2,1,0:T(2,128)S(1)} all-to-all(f32[128,2,256]{2,1,0:T(2,128)S(1)} %get-tuple-element.82), channel_id=1, replica_groups=mesh['lat'=32,'lon'=4] {'lat','lon'}, dimensions={0} | all-to-all | bytes 524288 | tf_op jit(solution)/shard_map/all_to_all | solution.py:262
  458.2 15.2 %all_to_all.137.refs_0_ = f32[128,2,256]{2,1,0:T(2,128)S(1)} all-to-all(f32[128,2,256]{2,1,0:T(2,128)S(1)} %legendre_pair.21), channel_id=1, replica_groups=mesh['lat'=32,'lon'=4] {'lat','lon'}, dimensions={0} | all-to-all | bytes 524288 | tf_op jit(solution)/shard_map/all_to_all | solution.py:275
  476.9 15.2 %all_to_all.138.refs_0_ = f32[128,2,256]{2,1,0:T(2,128)S(1)} all-to-all(f32[128,2,256]{2,1,0:T(2,128)S(1)} %get-tuple-element.86), channel_id=1, replica_groups=mesh['lat'=32,'lon'=4] {'lat','lon'}, dimensions={0} | all-to-all | bytes 524288 | tf_op jit(solution)/shard_map/all_to_all | solution.py:262
  496.3 15.5 %all_to_all.139.refs_0_ = f32[128,2,256]{2,1,0:T(2,128)S(1)} all-to-all(f32[128,2,256]{2,1,0:T(2,128)S(1)} %legendre_pair.22), channel_id=1, replica_groups=mesh['lat'=32,'lon'=4] {'lat','lon'}, dimensions={0} | all-to-all | bytes 524288 | tf_op jit(solution)/shard_map/all_to_all | solution.py:275
  515.2 15.2 %all_to_all.140.refs_0_ = f32[128,2,256]{2,1,0:T(2,128)S(1)} all-to-all(f32[128,2,256]{2,1,0:T(2,128)S(1)} %get-tuple-element.90), channel_id=1, replica_groups=mesh['lat'=32,'lon'=4] {'lat','lon'}, dimensions={0} | all-to-all | bytes 524288 | tf_op jit(solution)/shard_map/all_to_all | solution.py:262
  534.6 15.2 %all_to_all.141.refs_0_ = f32[128,2,256]{2,1,0:T(2,128)S(1)} all-to-all(f32[128,2,256]{2,1,0:T(2,128)S(1)} %legendre_pair.23), channel_id=1, replica_groups=mesh['lat'=32,'lon'=4] {'lat','lon'}, dimensions={0} | all-to-all | bytes 524288 | tf_op jit(solution)/shard_map/all_to_all | solution.py:275
  (185 shorter events, 191.5 us)
Async XLA Ops:
  2.2 9.6 %copy-start.46 = (s32[32]{0:T(128)S(1)}, s32[32]{0:T(128)}, u32[]{:S(2)}) copy-start(s32[32]{0:T(128)} %param.14) | copy-start | bytes 388
  3.6 49.5 %copy-start.21 = (f32[136,2304]{1,0:T(8,128)}, f32[136,2304]{1,0:T(8,128)S(1)}, u32[]{:S(2)}) copy-start(f32[136,2304]{1,0:T(8,128)S(1)} %convert_element_type.23) | copy-start | bytes 3760132
  9.2 10.2 %collective-permute-start.1 = (f32[5,136,128]{2,1,0:T(8,128)}, f32[5,136,128]{2,1,0:T(8,128)}, u32[]{:S(2)}, u32[]{:S(2)}) collective-permute-start(f32[5,136,128]{2,1,0:T(8,128)} %get-tuple-element.109), channel_id=1, source_target_pairs={{0,1},{1,2},{2,3},{3,0},{4,5},{5,6},{6,7},{7,4},{8,9},{9,10},{10,1... | collective-permute-start | bytes 1044488 | tf_op jit(solution)/shard_map/ppermute | solution.py:178
  11.8 8.9 %collective-permute-start = (f32[5,136,128]{2,1,0:T(8,128)}, f32[5,136,128]{2,1,0:T(8,128)}, u32[]{:S(2)}, u32[]{:S(2)}) collective-permute-start(f32[5,136,128]{2,1,0:T(8,128)} %get-tuple-element.110), channel_id=1, source_target_pairs={{0,3},{1,0},{2,1},{3,2},{4,7},{5,4},{6,5},{7,6},{8,11},{9,8},{10,9... | collective-permute-start | bytes 1044488 | tf_op jit(solution)/shard_map/ppermute | solution.py:178
  25.6 21.3 %collective-permute-start.2 = (f32[5,16,2432]{2,1,0:T(8,128)}, f32[5,16,2432]{2,1,0:T(8,128)}, u32[]{:S(2)}, u32[]{:S(2)}) collective-permute-start(f32[5,16,2432]{2,1,0:T(8,128)} %get-tuple-element.99), channel_id=1, source_target_pairs={{4,0},{8,4},{12,8},{16,12},{20,16},{24,20},{28,24},{32,28},{36,32}... | collective-permute-start | bytes 2334728 | tf_op jit(solution)/shard_map/ppermute | solution.py:184
  31.6 25.1 %copy-start.18 = (bf16[2304,128]{1,0:T(8,128)(2,1)}, bf16[2304,128]{1,0:T(8,128)(2,1)S(1)}, u32[]{:S(2)}) copy-start(bf16[2304,128]{1,0:T(8,128)(2,1)S(1)} %maximum_bitcast_fusion.refs_1_.refs_9_) | copy-start | bytes 1769476
  31.6 20.7 %collective-permute-start.3 = (f32[5,16,2432]{2,1,0:T(8,128)S(1)}, f32[5,16,2432]{2,1,0:T(8,128)S(1)}, u32[]{:S(2)}, u32[]{:S(2)}) collective-permute-start(f32[5,16,2432]{2,1,0:T(8,128)S(1)} %copy-done.43), channel_id=1, source_target_pairs={{0,4},{4,8},{8,12},{12,16},{16,20},{20,24},{24,28},{28,32},{32,36}... | collective-permute-start | bytes 2334728 | tf_op jit(solution)/shard_map/ppermute | solution.py:184
  56.7 17.9 %copy-start.35 = (f32[136,128]{1,0:T(8,128)S(1)}, f32[136,128]{1,0:T(8,128)}, u32[]{:S(2)}) copy-start(f32[136,128]{1,0:T(8,128)} %copy-done.34) | copy-start | bytes 208900
  56.7 17.9 %copy-start.40 = (f32[12,2432]{1,0:T(8,128)S(1)}, f32[12,2432]{1,0:T(8,128)}, u32[]{:S(2)}) copy-start(f32[12,2432]{1,0:T(8,128)} %get-tuple-element.122) | copy-start | bytes 350212
  56.7 17.9 %copy-start.41 = (f32[12,2432]{1,0:T(8,128)S(1)}, f32[12,2432]{1,0:T(8,128)}, u32[]{:S(2)}) copy-start(f32[12,2432]{1,0:T(8,128)} %get-tuple-element.127) | copy-start | bytes 350212
  58.1 27.7 %all-to-all-start = ((f32[128,2,256]{2,1,0:T(2,128)}), f32[128,2,256]{2,1,0:T(2,128)S(1)}, u32[]{:S(2)}, u32[]{:S(2)}) async-start(f32[128,2,256]{2,1,0:T(2,128)} %first_sums.1), calls=%async_computation | async-start | bytes 524288 | tf_op jit(solution)/shard_map/all_to_all | solution.py:262
  81.0 4.8 copy-start.45
  85.9 3.9 copy-start
  94.6 17.6 %all-to-all-start.1 = ((f32[128,2,256]{2,1,0:T(2,128)}), f32[128,2,256]{2,1,0:T(2,128)S(1)}, u32[]{:S(2)}, u32[]{:S(2)}) async-start(f32[128,2,256]{2,1,0:T(2,128)} %legendre_pair.12), calls=%async_computation.1 | async-start | bytes 524288 | tf_op jit(solution)/shard_map/all_to_all | solution.py:275
  100.9 11.4 %copy-start.3 = (f32[160,2432]{1,0:T(8,128)S(1)}, f32[160,2432]{1,0:T(8,128)}, u32[]{:S(2)}) copy-start(f32[160,2432]{1,0:T(8,128)} %copy-done.2) | copy-start | bytes 4669444
  121.6 44.7 %copy-start.11 = (f32[160,2432]{1,0:T(8,128)S(1)}, f32[160,2432]{1,0:T(8,128)}, u32[]{:S(2)}) copy-start(f32[160,2432]{1,0:T(8,128)} %pad_maximum_fusion.4.refs_4_) | copy-start | bytes 4669444
  121.6 44.7 %copy-start.13 = (f32[160,2432]{1,0:T(8,128)S(1)}, f32[160,2432]{1,0:T(8,128)}, u32[]{:S(2)}) copy-start(f32[160,2432]{1,0:T(8,128)} %get-tuple-element.97.refs_7_) | copy-start | bytes 4669444
  121.6 44.7 %copy-start.15 = (f32[160,2432]{1,0:T(8,128)S(1)}, f32[160,2432]{1,0:T(8,128)}, u32[]{:S(2)}) copy-start(f32[160,2432]{1,0:T(8,128)} %get-tuple-element.98.refs_6_) | copy-start | bytes 4669444
  121.6 44.7 %copy-start.20 = (bf16[2304,128]{1,0:T(8,128)(2,1)S(1)}, bf16[2304,128]{1,0:T(8,128)(2,1)}, u32[]{:S(2)}) copy-start(bf16[2304,128]{1,0:T(8,128)(2,1)} %copy-done.18) | copy-start | bytes 1769476
  146.5 19.9 %copy-start.6 = (f32[160,2432]{1,0:T(8,128)S(1)}, f32[160,2432]{1,0:T(8,128)}, u32[]{:S(2)}) copy-start(f32[160,2432]{1,0:T(8,128)} %copy-done.5) | copy-start | bytes 4669444
  146.5 19.9 %copy-start.17 = (bf16[256,2432]{1,0:T(8,128)(2,1)S(1)}, bf16[256,2432]{1,0:T(8,128)(2,1)}, u32[]{:S(2)}) copy-start(bf16[256,2432]{1,0:T(8,128)(2,1)} %copy.78.refs_8_) | copy-start | bytes 3735556
  146.5 39.9 %slice-start = ((s8[10027008]{0:T(1024)(128)(4,1)}), s8[4194304]{0:T(1024)(128)(4,1)S(1)}, s32[]{:S(2)}) async-start(s8[10027008]{0:T(1024)(128)(4,1)} %bitcast.99), calls=%async_computation.24 | async-start | bytes 8388608
  146.5 39.9 %slice-start.1 = ((s8[10027008]{0:T(1024)(128)(4,1)}), s8[4194304]{0:T(1024)(128)(4,1)S(1)}, s32[]{:S(2)}) async-start(s8[10027008]{0:T(1024)(128)(4,1)} %bitcast.99), calls=%async_computation.25 | async-start | bytes 8388608
  167.7 18.7 %slice-start.2 = ((s8[10027008]{0:T(1024)(128)(4,1)}), s8[1638400]{0:T(1024)(128)(4,1)S(1)}, s32[]{:S(2)}) async-start(s8[10027008]{0:T(1024)(128)(4,1)} %bitcast.99), calls=%async_computation.26 | async-start | bytes 3276800
  (33 other events, 65.7 us)

commit v2 on v1

v2 whole, which is shorter than its diff:
```python
import math

import jax
import jax.numpy as jnp
from jax import lax
from jax.experimental import pallas as pl
from jax.experimental.pallas import tpu as pltpu
from jax.sharding import PartitionSpec as P

STEPS = 12
HALO = STEPS
LANES = 128
SECOND = 192
MSG = 384
SLOT = 16

gravity_step = 0.12
volume_step = 0.12
retain_factor = 0.97

BOTH = ("lat", "lon")
VMEM = pl.BlockSpec(memory_space=pltpu.VMEM)
HIGH = jnp.float32
LOW = jnp.bfloat16


def in_vmem(value):
    return pltpu.with_memory_space_constraint(value, pltpu.VMEM)


def in_hbm(value):
    return pltpu.with_memory_space_constraint(value, pltpu.HBM)


def lanes_of(shape):
    return lax.broadcasted_iota(jnp.int32, shape, 1)


def rows_of(shape):
    return lax.broadcasted_iota(jnp.int32, shape, 0)


def split_pair(value):
    high = value.astype(LOW)
    return high, (value - high.astype(HIGH)).astype(LOW)


def received(got_ref, line_ref):
    every = got_ref.shape[0]
    count = every // 4
    tiles = []
    for tile in range(MSG // LANES):
        base = tile * every
        line_ref[base : base + every, :] = got_ref[:, tile * LANES : (tile + 1) * LANES]
        total = line_ref[pl.ds(base, count, stride=4), :]
        for part in range(1, 4):
            total = total + line_ref[pl.ds(base + part, count, stride=4), :]
        tiles.append(total)
    return jnp.concatenate(tiles, axis=1)


def send(message, out_ref, line_ref):
    every = out_ref.shape[0]
    for tile in range(MSG // LANES):
        base, block = tile * every, slice(tile * LANES, (tile + 1) * LANES)
        for part in range(4):
            line_ref[pl.ds(base + part, every // 4, stride=4), :] = message[:, block]
        out_ref[:, block] = line_ref[base : base + every, :]


def second_part(message):
    return pltpu.roll(message[:, LANES:], 2 * LANES - (SECOND - LANES), 1)


def fourier_sums(rows, read, table_ref, out_ref, line_ref):
    cols = table_ref.shape[0]
    total = jnp.zeros((2 * rows, LANES), HIGH)
    for start in range(0, cols, 256):
        high, low = split_pair(read(start))
        both = jnp.concatenate([high, low], axis=0)
        total = total + jnp.dot(both, table_ref[start : start + 256, :], preferred_element_type=HIGH)
    half = total[:rows] + total[rows:]
    half = half + pltpu.roll(half, LANES // 2, 1)
    half = jnp.concatenate([half, jnp.zeros((256 - rows, LANES), HIGH)], axis=0)
    sums = jnp.transpose(half)
    slots = out_ref.shape[0] // 4
    first = sums[:slots]
    second = pltpu.roll(sums[slots : 2 * slots], SECOND - LANES, 1)
    middle = jnp.where(lanes_of((slots, LANES)) < SECOND - LANES, first[:, LANES:], second[:, :LANES])
    send(jnp.concatenate([first[:, :LANES], middle, second[:, LANES:]], axis=1), out_ref, line_ref)


def first_kernel(rows, height_ref, basis_ref, out_ref, table_ref, synth_ref, line_ref):
    own, cols = height_ref.shape
    basis = basis_ref[...]
    high, low = split_pair(basis)
    count = basis.shape[0]
    synth_ref[:count, :] = high
    synth_ref[count : 2 * count, :] = low
    synth_ref[2 * count : 3 * count, :] = high
    synth_ref[3 * count :, :] = jnp.zeros_like(high)
    for start in range(0, cols, LANES):
        block = slice(start, start + LANES)
        both = jnp.concatenate([high[:, block].astype(HIGH), low[:, block].astype(HIGH)], axis=0)
        table_ref[block, :] = jnp.transpose(both).astype(LOW)

    def read(start):
        block = height_ref[:, start : start + 256]
        return jnp.concatenate([block, jnp.zeros((rows - own, 256), HIGH)], axis=0)

    fourier_sums(rows, read, table_ref, out_ref, line_ref)


def above_of(ref, start, tall):
    if start + 8 < tall:
        return ref[start + 1 : start + 9, :]
    return jnp.concatenate([ref[start + 1 : tall, :], ref[:1, :]], axis=0)


def grid_kernel(rows, last, *refs):
    (got_ref, level_in, east_in, north_in, bathy_ref, wet_ref, east_open_ref, north_open_ref) = refs[:8]
    synth_ref, refs = refs[8], refs[9:]
    if last:
        level_ref, east_ref, north_ref, pot_ref, depth_ref, south_ref, line_ref = refs
    else:
        table_ref, level_ref, east_ref, north_ref, out_ref = refs[:5]
        pot_ref, depth_ref, south_ref, line_ref = refs[5:]
    tall, wide = level_in.shape
    own, cols = level_ref.shape
    message = received(got_ref, line_ref)
    slots = message.shape[0]
    back = jnp.concatenate([message[:, : 2 * LANES], second_part(message)], axis=0)
    back = back * (1.0 / math.sqrt(4 * (wide - LANES)))
    back = jnp.where(
        lanes_of(back.shape) < tall - HALO,
        pltpu.roll(back, 2 * LANES - HALO, 1),
        pltpu.roll(back, tall - HALO, 1),
    )
    high, low = split_pair(back)
    high, low = high.astype(HIGH), low.astype(HIGH)
    stacked = jnp.concatenate([high, high, low, jnp.zeros_like(low)], axis=0)
    factors = jnp.transpose(stacked)[:tall].astype(LOW)
    half_gravity = gravity_step * 0.5
    for start in range(0, wide, 256):
        block = slice(start, min(start + 256, wide))
        pull = jnp.dot(factors, synth_ref[:, block], preferred_element_type=HIGH)
        level = level_in[:, block]
        pot_ref[:tall, block] = level + pull
        depth_ref[:tall, block] = (half_gravity * wet_ref[:, block]) * jnp.maximum(
            bathy_ref[:, block] + level, 0.0
        )
    pot_ref[tall:, :] = pot_ref[:8, :]
    depth_ref[tall:, :] = depth_ref[:8, :]

    def update(start):
        here = slice(start, start + 8)
        above = slice(start + 1, start + 9)
        pot, depth = pot_ref[here, :], depth_ref[here, :]
        pot_east, depth_east = pltpu.roll(pot, wide - 1, 1), pltpu.roll(depth, wide - 1, 1)
        east = east_open_ref[here, :] * (
            east_in[here, :] - (depth + depth_east) * (pot_east - pot)
        )
        north = north_open_ref[here, :] * (
            north_in[here, :] - (depth + depth_ref[above, :]) * (pot_ref[above, :] - pot)
        )
        south_ref[start + 8 : start + 16, :] = north
        below = south_ref[start + 7 : start + 15, :]
        level = level_in[here, :] - (volume_step * wet_ref[here, :]) * (
            east - pltpu.roll(east, 1, 1) + north - below
        )
        if start < own:
            east_ref[here, :] = east[:, :cols]
            north_ref[here, :] = north[:, :cols]
            level_ref[here, :] = level[:, :cols]

    if last:
        update(tall - 8)
        south_ref[:8, :] = south_ref[tall : tall + 8, :]
        for start in range(0, own, 8):
            update(start)
    else:
        seam = tall - 2 * HALO
        south_ref[seam : seam + 8, :] = jnp.zeros((8, wide), HIGH)
        for start in range(seam, tall, 8):
            update(start)
        south_ref[:8, :] = south_ref[tall : tall + 8, :]
        for start in range(0, seam, 8):
            update(start)
        fix = slice(seam, seam + 8)
        row = rows_of((8, wide))
        missed = jnp.where(row == 0, south_ref[seam + 7 : seam + 15, :], 0.0)
        level_ref[fix, :] = level_ref[fix, :] + (volume_step * wet_ref[fix, :]) * missed
        def read(start):
            return level_ref[:rows, start : start + 256]

        fourier_sums(rows, read, table_ref, out_ref, line_ref)


def legendre_kernel(band, first, got_ref, legendre_ref, weight_ref, love_ref, *refs):
    if first:
        out_ref, held_ref, tiles_ref, line_ref, copies = refs
    else:
        out_ref, tiles_ref, line_ref = refs
        held_ref = legendre_ref
    total, degrees = legendre_ref.shape
    bands = total // band
    count = total // LANES
    chunk = 2 * LANES
    step = band - LANES

    def copy(start):
        block = pl.ds(start, chunk)
        return pltpu.make_async_copy(
            legendre_ref.at[block, :], held_ref.at[block, :], copies.at[start // chunk]
        )

    if first:
        for start in range(0, total, chunk):
            copy(start).start()

    message = received(got_ref, line_ref)
    tall = tiles_ref.shape[0] // 2
    for k, part in enumerate((message[:, :chunk], second_part(message))):
        part = jnp.where(lanes_of(part.shape) < band, part, 0.0)
        part = pltpu.roll(part, 0, 1, stride=step, stride_axis=0)
        early, late = part[:, :LANES], part[:, LANES:]
        zeros = jnp.zeros((tall - bands, LANES), HIGH)
        row = rows_of((tall, LANES))
        early = jnp.concatenate([early, zeros], axis=0)
        late = jnp.concatenate([late, zeros], axis=0)
        wraps = LANES // step
        line = (
            pltpu.roll(late, 1, 0)
            + jnp.where(row < wraps, early, 0.0)
            + jnp.where(row >= wraps + 2, pltpu.roll(early, 2, 0), 0.0)
        )
        tiles_ref[k * tall : (k + 1) * tall, :] = line * weight_ref[...]
    coeff = jnp.zeros((2, degrees), HIGH)
    for start in range(0, total, chunk):
        tile = start // LANES
        weighted = jnp.concatenate(
            [tiles_ref[pl.ds(tile + i, 2, stride=tall), :] for i in range(2)], axis=1
        ).astype(LOW)
        if first:
            copy(start).wait()
        coeff = coeff + jnp.dot(
            weighted, held_ref[start : start + chunk, :], preferred_element_type=HIGH
        )
    scaled = (coeff * love_ref[...]).astype(LOW)
    tiles_ref[...] = jnp.zeros_like(tiles_ref)
    for start in range(0, total, chunk):
        back = lax.dot_general(
            scaled,
            held_ref[start : start + chunk, :],
            (((1,), (1,)), ((), ())),
            preferred_element_type=HIGH,
        )
        row = tall - 2 - start // LANES
        for i in range(2):
            tiles_ref[pl.ds(row - i, 2, stride=tall), :] = back[:, i * LANES : (i + 1) * LANES]
    parts = []
    reach = LANES - HALO + step * (bands - 1 - rows_of((bands, LANES)))
    for k in range(2):

        def tile(shift):
            begin = (k + 1) * tall - bands - shift
            return tiles_ref[begin : begin + bands, :]

        window = jnp.concatenate(
            [
                jnp.where(reach < LANES, tile(0), tile(3)),
                jnp.where(reach < 2 * LANES, tile(1), tile(4)),
                tile(2),
            ],
            axis=1,
        )
        shift = (k * SECOND - LANES + HALO - step * (bands - 1)) % MSG
        window = pltpu.roll(window, shift, 1)
        parts.append(pltpu.roll(window, 0, 1, stride=step, stride_axis=0))
    result = jnp.where(lanes_of(parts[0].shape) < SECOND, parts[0], parts[1])
    for index in range(bands):
        at = bands - 1 - index
        out_ref[4 * index : 4 * index + 4, :] = jnp.broadcast_to(result[at : at + 1, :], (4, MSG))


def ghost_tile(index, east, west):
    lane = lanes_of(east.shape)
    east = pltpu.roll(east, LANES - SLOT * index, 1) if index else east
    west = pltpu.roll(west, LANES - SLOT * (index + 1), 1)
    return jnp.where(lane < HALO, east, jnp.where(lane >= LANES - HALO, west, 0.0))


def column_edge_kernel(*refs):
    fields, (west_ref, east_ref) = refs[:-2], refs[-2:]
    lane = lanes_of(west_ref.shape)
    west = jnp.zeros(west_ref.shape, HIGH)
    east = jnp.zeros(east_ref.shape, HIGH)
    for index in range(len(fields) // 2):
        left, right = (ref[...].astype(HIGH) for ref in fields[2 * index : 2 * index + 2])
        here = (lane >= SLOT * index) & (lane < SLOT * (index + 1))
        west = jnp.where(here, pltpu.roll(left, SLOT * index, 1) if index else left, west)
        east = jnp.where(here, pltpu.roll(right, SLOT * (index + 1), 1), east)
    west_ref[...] = west
    east_ref[...] = east


def row_edge_kernel(begin, *refs):
    fields, (from_east, from_west, unused_ref, out_ref) = refs[:-4], refs[-4:]
    cols = fields[0].shape[1]
    keep = slice(begin, begin + HALO)
    out_ref[len(fields) // 2 * HALO :, :] = jnp.zeros_like(out_ref[len(fields) // 2 * HALO :, :])
    for index in range(len(fields) // 2):
        both = jnp.concatenate([ref[...].astype(HIGH) for ref in fields[2 * index : 2 * index + 2]], axis=0)
        where = slice(HALO * index, HALO * (index + 1))
        out_ref[where, :cols] = both[keep]
        out_ref[where, cols:] = ghost_tile(index, from_east[...], from_west[...])[keep]


def assemble_kernel(*refs):
    fields, refs = refs[:5], refs[5:]
    (from_east, from_west, from_north, from_south), refs = refs[:4], refs[4:]
    outs, (east_open_ref, north_open_ref, mask_ref, copies) = refs[:5], refs[5:]
    rows, cols = fields[0].shape
    tall, wide = outs[0].shape
    targets = [out.at[:rows, :cols] for out in outs[:4]] + [mask_ref]
    moves = [
        pltpu.make_async_copy(field, target, copies.at[index])
        for index, (field, target) in enumerate(zip(fields, targets))
    ]
    for move in moves[::-1]:
        move.start()
    for index, out in enumerate(outs):
        out[:rows, cols:] = ghost_tile(index, from_east[...], from_west[...])
        begin = HALO * index
        out[rows:, :] = jnp.concatenate(
            [from_north[begin : begin + HALO, :], from_south[begin : begin + HALO, :]], axis=0
        )
    moves[4].wait()
    wet_ref = outs[4]
    wet_ref[:rows, :cols] = mask_ref[...].astype(HIGH)
    for start in range(0, tall, 8):
        here = slice(start, start + 8)
        wet = wet_ref[here, :]
        above = above_of(wet_ref, start, tall)
        if start <= rows + HALO - 1 < start + 8:
            above = jnp.where(rows_of(above.shape) == rows + HALO - 1 - start, 0.0, above)
        east_open_ref[here, :] = retain_factor * wet * pltpu.roll(wet, wide - 1, 1)
        north_open_ref[here, :] = retain_factor * wet * above
    for move in moves[:4]:
        move.wait()


def shifted(value, axis, by):
    count = lax.axis_size(axis)
    return lax.ppermute(value, axis, [(i, (i + by) % count) for i in range(count)])


def shifted_open(value, axis, by):
    count = lax.axis_size(axis)
    pairs = [(i, i + by) for i in range(count) if 0 <= i + by < count]
    return lax.ppermute(value, axis, pairs)


def shards(
    height,
    flux_east,
    flux_north,
    bathymetry,
    wet_mask,
    wavenumber,
    legendre,
    quadrature,
    love_factor,
):
    lon_count = lax.axis_size("lon")
    lat_count = lax.axis_size("lat")
    rows, cols = height.shape
    slots = wavenumber.shape[0]
    total_cols = cols * lon_count
    total_rows = rows * lat_count
    tall, wide = rows + 2 * HALO, cols + LANES
    devices = lat_count * lon_count
    padded_rows = -(-rows // 16) * 16
    legendre = legendre.reshape(legendre.shape[1:])
    degrees = legendre.shape[1]
    small = pltpu.CompilerParams(vmem_limit_bytes=12 * 2**20)
    message = jax.ShapeDtypeStruct((devices, MSG), HIGH)
    field = jax.ShapeDtypeStruct((tall, wide), HIGH)
    line = pltpu.VMEM((MSG // LANES * devices, LANES), HIGH)
    fields = [height, flux_east, flux_north, bathymetry, wet_mask]

    column_edge = jax.ShapeDtypeStruct((rows, LANES), HIGH)
    edge_spec = pl.BlockSpec((rows, LANES), lambda i: (0, 0))
    west_edge, east_edge = pl.pallas_call(
        column_edge_kernel,
        grid=(1,),
        out_shape=(column_edge,) * 2,
        in_specs=[edge_spec, pl.BlockSpec((rows, LANES), lambda i: (0, cols // LANES - 1))] * 5,
        out_specs=(edge_spec,) * 2,
        compiler_params=small,
        name="column_edges",
    )(*[in_hbm(f) for f in fields for _ in range(2)])
    from_east = shifted(west_edge, "lon", -1)
    from_west = shifted(east_edge, "lon", 1)

    def row_edge(start, keep, after):
        block = [pl.BlockSpec((8, cols), lambda i, at=start // 8 + n: (at, 0)) for n in range(2)]
        ghost = pl.BlockSpec((16, LANES), lambda i: (0, 0))
        return pl.pallas_call(
            lambda *refs: row_edge_kernel(keep, *refs),
            grid=(1,),
            out_shape=jax.ShapeDtypeStruct((64, wide), HIGH),
            in_specs=block * 5 + [ghost, ghost, pl.BlockSpec(memory_space=pl.ANY)],
            out_specs=pl.BlockSpec((64, wide), lambda i: (0, 0)),
            compiler_params=small,
            name="row_edges",
        )(
            *[in_hbm(f) for f in fields for _ in range(2)],
            from_east[start : start + 16],
            from_west[start : start + 16],
            after,
        )

    lane = jnp.arange(wide, dtype=jnp.int32)
    offset = jnp.where(lane < cols + LANES // 2, lane, lane - wide)
    columns = (lax.axis_index("lon") * cols + offset + total_cols) % total_cols
    product = wavenumber[:, None] * columns[None, :] % total_cols
    angle = product.astype(HIGH) * (2.0 * math.pi / total_cols)
    basis = jnp.concatenate([jnp.cos(angle), -jnp.sin(angle)], axis=0)
    weight = (quadrature / math.sqrt(total_cols)).reshape(total_rows // LANES, LANES)
    weight = jnp.pad(weight, ((0, 40 - total_rows // LANES), (0, 0)))
    love = love_factor[None, :]

    sums, table, synth = pl.pallas_call(
        lambda *refs: first_kernel(padded_rows, *refs),
        out_shape=(
            message,
            pltpu.VMEM((cols, LANES), LOW),
            pltpu.VMEM((8 * slots, wide), LOW),
        ),
        in_specs=[VMEM] * 2,
        out_specs=(VMEM,) * 3,
        scratch_shapes=[line],
        compiler_params=small,
        name="first_sums",
    )(height, basis)

    held = pltpu.VMEM((tall, wide), HIGH)
    tiles = pltpu.VMEM((80, LANES), HIGH)
    for step in range(STEPS):
        first, last = step == 0, step == STEPS - 1
        spectral = lax.all_to_all(sums, BOTH, split_axis=0, concat_axis=0, tiled=True)
        if first:
            back, legendre = pl.pallas_call(
                lambda *refs: legendre_kernel(rows, True, *refs),
                out_shape=(message, pltpu.VMEM(legendre.shape, LOW)),
                in_specs=[VMEM, pl.BlockSpec(memory_space=pl.ANY), VMEM, VMEM],
                out_specs=(VMEM,) * 2,
                scratch_shapes=[tiles, line, pltpu.SemaphoreType.DMA((total_rows // 256,))],
                compiler_params=small,
                name="legendre_first",
            )(spectral, in_hbm(legendre), weight, love)
        else:
            back = pl.pallas_call(
                lambda *refs: legendre_kernel(rows, False, *refs),
                out_shape=message,
                in_specs=[VMEM] * 4,
                out_specs=VMEM,
                scratch_shapes=[tiles, line],
                compiler_params=small,
                name="legendre_pair",
            )(spectral, in_vmem(legendre), in_vmem(weight), in_vmem(love))
        if first:
            from_north = shifted_open(row_edge(0, 0, spectral), "lat", -1)
            from_south = shifted_open(row_edge(rows - 16, 16 - HALO, back), "lat", 1)
            level, east, north, bathy, wet, east_open, north_open = pl.pallas_call(
                assemble_kernel,
                out_shape=(held,) * 7,
                in_specs=[pl.BlockSpec(memory_space=pl.ANY)] * 5 + [VMEM] * 4,
                out_specs=(VMEM,) * 7,
                scratch_shapes=[pltpu.VMEM((rows, cols), jnp.int32), pltpu.SemaphoreType.DMA((5,))],
                compiler_params=small,
                name="assemble",
            )(*[in_hbm(f) for f in fields], from_east, from_west, from_north, from_south)
        bands = lax.all_to_all(back, BOTH, split_axis=0, concat_axis=0, tiled=True)
        operands = [bands] + [
            in_vmem(x) for x in (level, east, north, bathy, wet, east_open, north_open, synth, table)
        ]
        scratch = [pltpu.VMEM((tall + 8, wide), HIGH)] * 3 + [line]
        if last:
            own = jax.ShapeDtypeStruct((rows, cols), HIGH)
            return pl.pallas_call(
                lambda *refs: grid_kernel(padded_rows, True, *refs),
                out_shape=(own,) * 3,
                in_specs=[VMEM] * 9,
                out_specs=(VMEM,) * 3,
                scratch_shapes=scratch,
                compiler_params=small,
                name="grid_last",
            )(*operands[:9])
        level, east, north, sums = pl.pallas_call(
            lambda *refs: grid_kernel(padded_rows, False, *refs),
            out_shape=(field, field, field, message),
            in_specs=[VMEM] * 10,
            out_specs=(VMEM,) * 4,
            scratch_shapes=scratch,
            input_output_aliases={1: 0, 2: 1, 3: 2},
            compiler_params=small,
            name="grid_update",
        )(*operands)


def solution(mesh):
    placed = (
        P("lat", "lon"),
        P("lat", "lon"),
        P("lat", "lon"),
        P("lat", "lon"),
        P("lat", "lon"),
        P(),
        P("lat", None, "lon"),
        P(),
        P("lon"),
    )
    return jax.shard_map(
        shards,
        mesh=mesh,
        in_specs=placed,
        out_specs=(P("lat", "lon"), P("lat", "lon"), P("lat", "lon")),
        check_vma=False,
    )
```

time: 565 us -> 503 us (0.89)
  local copies, waits for them, and re-layouts: 44.1 us -> 5.94 us
  other arithmetic: 22.4 us -> 1.41 us
  waiting for transfers between devices: 28.1 us -> 10.7 us
  Pallas kernels: 93.9 us -> 109 us
  starting transfers between devices: 30.6 us -> 18.1 us
  blocking collectives: 337 us -> 349 us
    unnamed x104 -> x32, local copies, waits for them, and re-layouts: 27.8 us -> 0.35 us
    pallas_call x24 -> x28, Pallas kernels: 92.5 us -> 108 us  [the longest x11 48.1 us: shards(): pl.pallas_call(lambda *refs: legendre_kernel(rows, False, *refs), out_sha...]
    ppermute x2, waiting for transfers between devices: 14.6 us -> 0.01 us  [shifted_open(): return lax.ppermute(value, axis, pairs)]
    all_to_all x2 -> x1, starting transfers between devices: 22.7 us -> 10 us  [shards(): lax.all_to_all(sums, BOTH, split_axis=0, concat_axis=0, tiled=True)]
    all_to_all x22 -> x23, blocking collectives: 337 us -> 349 us  [the longest x12 185 us: shards(): bands = lax.all_to_all(back, BOTH, split_axis=0, concat_axis=0, tiled=True)]
    concatenate x6 -> x1, other arithmetic: 7.91 us -> 0.05 us  [shards(): basis = jnp.concatenate([jnp.cos(angle), -jnp.sin(angle)], axis=0)]
    slice x9 -> x2, local copies, waits for them, and re-layouts: 7.34 us -> 0.01 us  [the longest x1 0.01 us: row_edge(): from_west[start:start + 16]]
    all_to_all x2 -> x1, waiting for transfers between devices: 12 us -> 10.6 us  [shards(): lax.all_to_all(sums, BOTH, split_axis=0, concat_axis=0, tiled=True)]
  transfers between devices with their start and end apart: 6 -> 5, of which waited for: 6 -> 1; matrix products, arithmetic and copies ran while one was open for 4% -> 1% of each run, Pallas kernels for 0% -> 2%
where the time goes in v2:
time: 503 us; the launch traced here: 496 us
  blocking collectives  349 us (69%)
  Pallas kernels  109 us (22%)
  starting transfers between devices  18.1 us (4%)
  waiting for transfers between devices  10.7 us (2%)
  local copies, waits for them, and re-layouts  5.94 us (1%)
    all_to_all x12, blocking collectives, shards(): bands = lax.all_to_all(back, BOTH, split_axis=0, concat_axis=0, tiled=True)  185 us
    all_to_all x11, blocking collectives, shards(): lax.all_to_all(sums, BOTH, split_axis=0, concat_axis=0, tiled=True)  164 us
    pallas_call x11, Pallas kernels, shards(): pl.pallas_call(lambda *refs: legendre_kernel(rows, False, *refs), out_sha...  48.1 us
    pallas_call x11, Pallas kernels, shards(): pl.pallas_call(lambda *refs: grid_kernel(padded_rows, False, *refs), out_...  40.9 us
    all_to_all x1, waiting for transfers between devices, shards(): lax.all_to_all(sums, BOTH, split_axis=0, concat_axis=0, tiled=True)  10.6 us
  transfers between devices with their start and end apart: 5, of which 1 were waited for; matrix products, arithmetic and copies ran while one was open for 1% of the time, Pallas kernels for 2%

profile of v2, /device:TPU:1, one launch (start us, length us, event | category | flops | bytes accessed | tf_op | source)
XLA Modules:
  0.0 495.7 jit_solution(2990584426820084698)
XLA Ops:
  18.3 10.6 %all-to-all-done = f32[128,1,384]{2,1,0:T(1,128)S(1)} async-done(((f32[128,1,384]{2,1,0:T(1,128)}), f32[128,1,384]{2,1,0:T(1,128)S(1)}, u32[]{:S(2)}, u32[]{:S(2)}) %all-to-all-start) | async-done | bytes 196640 | tf_op jit(solution)/shard_map/all_to_all | solution.py:452
  44.6 23.3 %all_to_all.264 = f32[128,1,384]{2,1,0:T(1,128)S(1)} all-to-all(f32[128,1,384]{2,1,0:T(1,128)S(1)} %copy.46), channel_id=1, replica_groups=mesh['lat'=32,'lon'=4] {'lat','lon'}, dimensions={0} | all-to-all | bytes 393216 | tf_op jit(solution)/shard_map/all_to_all | solution.py:485
  74.8 16.6 %all_to_all.265 = f32[128,1,384]{2,1,0:T(1,128)S(1)} all-to-all(f32[128,1,384]{2,1,0:T(1,128)S(1)} %copy.47), channel_id=1, replica_groups=mesh['lat'=32,'lon'=4] {'lat','lon'}, dimensions={0} | all-to-all | bytes 393216 | tf_op jit(solution)/shard_map/all_to_all | solution.py:452
  96.0 15.1 %all_to_all.266 = f32[128,1,384]{2,1,0:T(1,128)S(1)} all-to-all(f32[128,1,384]{2,1,0:T(1,128)S(1)} %copy.48), channel_id=1, replica_groups=mesh['lat'=32,'lon'=4] {'lat','lon'}, dimensions={0} | all-to-all | bytes 393216 | tf_op jit(solution)/shard_map/all_to_all | solution.py:485
  115.1 14.6 %all_to_all.267 = f32[128,1,384]{2,1,0:T(1,128)S(1)} all-to-all(f32[128,1,384]{2,1,0:T(1,128)S(1)} %copy.49), channel_id=1, replica_groups=mesh['lat'=32,'lon'=4] {'lat','lon'}, dimensions={0} | all-to-all | bytes 393216 | tf_op jit(solution)/shard_map/all_to_all | solution.py:452
  134.3 14.6 %all_to_all.268 = f32[128,1,384]{2,1,0:T(1,128)S(1)} all-to-all(f32[128,1,384]{2,1,0:T(1,128)S(1)} %copy.50), channel_id=1, replica_groups=mesh['lat'=32,'lon'=4] {'lat','lon'}, dimensions={0} | all-to-all | bytes 393216 | tf_op jit(solution)/shard_map/all_to_all | solution.py:485
  152.9 14.8 %all_to_all.269 = f32[128,1,384]{2,1,0:T(1,128)S(1)} all-to-all(f32[128,1,384]{2,1,0:T(1,128)S(1)} %copy.51), channel_id=1, replica_groups=mesh['lat'=32,'lon'=4] {'lat','lon'}, dimensions={0} | all-to-all | bytes 393216 | tf_op jit(solution)/shard_map/all_to_all | solution.py:452
  172.3 14.6 %all_to_all.270 = f32[128,1,384]{2,1,0:T(1,128)S(1)} all-to-all(f32[128,1,384]{2,1,0:T(1,128)S(1)} %copy.52), channel_id=1, replica_groups=mesh['lat'=32,'lon'=4] {'lat','lon'}, dimensions={0} | all-to-all | bytes 393216 | tf_op jit(solution)/shard_map/all_to_all | solution.py:485
  190.9 14.6 %all_to_all.271 = f32[128,1,384]{2,1,0:T(1,128)S(1)} all-to-all(f32[128,1,384]{2,1,0:T(1,128)S(1)} %copy.53), channel_id=1, replica_groups=mesh['lat'=32,'lon'=4] {'lat','lon'}, dimensions={0} | all-to-all | bytes 393216 | tf_op jit(solution)/shard_map/all_to_all | solution.py:452
  210.1 14.9 %all_to_all.272 = f32[128,1,384]{2,1,0:T(1,128)S(1)} all-to-all(f32[128,1,384]{2,1,0:T(1,128)S(1)} %copy.54), channel_id=1, replica_groups=mesh['lat'=32,'lon'=4] {'lat','lon'}, dimensions={0} | all-to-all | bytes 393216 | tf_op jit(solution)/shard_map/all_to_all | solution.py:485
  228.9 14.6 %all_to_all.273 = f32[128,1,384]{2,1,0:T(1,128)S(1)} all-to-all(f32[128,1,384]{2,1,0:T(1,128)S(1)} %copy.55), channel_id=1, replica_groups=mesh['lat'=32,'lon'=4] {'lat','lon'}, dimensions={0} | all-to-all | bytes 393216 | tf_op jit(solution)/shard_map/all_to_all | solution.py:452
  248.2 14.6 %all_to_all.274 = f32[128,1,384]{2,1,0:T(1,128)S(1)} all-to-all(f32[128,1,384]{2,1,0:T(1,128)S(1)} %copy.56), channel_id=1, replica_groups=mesh['lat'=32,'lon'=4] {'lat','lon'}, dimensions={0} | all-to-all | bytes 393216 | tf_op jit(solution)/shard_map/all_to_all | solution.py:485
  266.7 15.1 %all_to_all.275 = f32[128,1,384]{2,1,0:T(1,128)S(1)} all-to-all(f32[128,1,384]{2,1,0:T(1,128)S(1)} %copy.57), channel_id=1, replica_groups=mesh['lat'=32,'lon'=4] {'lat','lon'}, dimensions={0} | all-to-all | bytes 393216 | tf_op jit(solution)/shard_map/all_to_all | solution.py:452
  286.4 14.6 %all_to_all.276 = f32[128,1,384]{2,1,0:T(1,128)S(1)} all-to-all(f32[128,1,384]{2,1,0:T(1,128)S(1)} %copy.58), channel_id=1, replica_groups=mesh['lat'=32,'lon'=4] {'lat','lon'}, dimensions={0} | all-to-all | bytes 393216 | tf_op jit(solution)/shard_map/all_to_all | solution.py:485
  305.0 14.6 %all_to_all.277 = f32[128,1,384]{2,1,0:T(1,128)S(1)} all-to-all(f32[128,1,384]{2,1,0:T(1,128)S(1)} %copy.59), channel_id=1, replica_groups=mesh['lat'=32,'lon'=4] {'lat','lon'}, dimensions={0} | all-to-all | bytes 393216 | tf_op jit(solution)/shard_map/all_to_all | solution.py:452
  324.2 14.8 %all_to_all.278 = f32[128,1,384]{2,1,0:T(1,128)S(1)} all-to-all(f32[128,1,384]{2,1,0:T(1,128)S(1)} %copy.60), channel_id=1, replica_groups=mesh['lat'=32,'lon'=4] {'lat','lon'}, dimensions={0} | all-to-all | bytes 393216 | tf_op jit(solution)/shard_map/all_to_all | solution.py:485
  343.0 14.6 %all_to_all.279 = f32[128,1,384]{2,1,0:T(1,128)S(1)} all-to-all(f32[128,1,384]{2,1,0:T(1,128)S(1)} %copy.61), channel_id=1, replica_groups=mesh['lat'=32,'lon'=4] {'lat','lon'}, dimensions={0} | all-to-all | bytes 393216 | tf_op jit(solution)/shard_map/all_to_all | solution.py:452
  362.2 14.6 %all_to_all.280 = f32[128,1,384]{2,1,0:T(1,128)S(1)} all-to-all(f32[128,1,384]{2,1,0:T(1,128)S(1)} %copy.62), channel_id=1, replica_groups=mesh['lat'=32,'lon'=4] {'lat','lon'}, dimensions={0} | all-to-all | bytes 393216 | tf_op jit(solution)/shard_map/all_to_all | solution.py:485
  380.8 14.9 %all_to_all.281 = f32[128,1,384]{2,1,0:T(1,128)S(1)} all-to-all(f32[128,1,384]{2,1,0:T(1,128)S(1)} %copy.63), channel_id=1, replica_groups=mesh['lat'=32,'lon'=4] {'lat','lon'}, dimensions={0} | all-to-all | bytes 393216 | tf_op jit(solution)/shard_map/all_to_all | solution.py:452
  400.3 14.6 %all_to_all.282 = f32[128,1,384]{2,1,0:T(1,128)S(1)} all-to-all(f32[128,1,384]{2,1,0:T(1,128)S(1)} %copy.64), channel_id=1, replica_groups=mesh['lat'=32,'lon'=4] {'lat','lon'}, dimensions={0} | all-to-all | bytes 393216 | tf_op jit(solution)/shard_map/all_to_all | solution.py:485
  418.9 14.6 %all_to_all.283 = f32[128,1,384]{2,1,0:T(1,128)S(1)} all-to-all(f32[128,1,384]{2,1,0:T(1,128)S(1)} %copy.65), channel_id=1, replica_groups=mesh['lat'=32,'lon'=4] {'lat','lon'}, dimensions={0} | all-to-all | bytes 393216 | tf_op jit(solution)/shard_map/all_to_all | solution.py:452
  438.1 14.9 %all_to_all.284 = f32[128,1,384]{2,1,0:T(1,128)S(1)} all-to-all(f32[128,1,384]{2,1,0:T(1,128)S(1)} %copy.66), channel_id=1, replica_groups=mesh['lat'=32,'lon'=4] {'lat','lon'}, dimensions={0} | all-to-all | bytes 393216 | tf_op jit(solution)/shard_map/all_to_all | solution.py:485
  457.0 14.6 %all_to_all.285 = f32[128,1,384]{2,1,0:T(1,128)S(1)} all-to-all(f32[128,1,384]{2,1,0:T(1,128)S(1)} %copy.67), channel_id=1, replica_groups=mesh['lat'=32,'lon'=4] {'lat','lon'}, dimensions={0} | all-to-all | bytes 393216 | tf_op jit(solution)/shard_map/all_to_all | solution.py:452
  476.2 14.6 %all_to_all.286 = f32[128,1,384]{2,1,0:T(1,128)S(1)} all-to-all(f32[128,1,384]{2,1,0:T(1,128)S(1)} %copy.68), channel_id=1, replica_groups=mesh['lat'=32,'lon'=4] {'lat','lon'}, dimensions={0} | all-to-all | bytes 393216 | tf_op jit(solution)/shard_map/all_to_all | solution.py:485
  (102 shorter events, 134.3 us)
Async XLA Ops:
  0.6 4.2 copy-start.3
  2.1 4.2 copy-start
  2.1 16.1 %collective-permute-start = (f32[136,128]{1,0:T(8,128)S(1)}, f32[136,128]{1,0:T(8,128)S(1)}, u32[]{:S(2)}, u32[]{:S(2)}) collective-permute-start(f32[136,128]{1,0:T(8,128)S(1)} %get-tuple-element.63), channel_id=1, source_target_pairs={{0,3},{1,0},{2,1},{3,2},{4,7},{5,4},{6,5},{7,6},{8,11},{9,8},{10,9... | collective-permute-start | bytes 208904 | tf_op jit(solution)/shard_map/ppermute | solution.py:355
  3.6 14.7 %collective-permute-start.1 = (f32[136,128]{1,0:T(8,128)S(1)}, f32[136,128]{1,0:T(8,128)S(1)}, u32[]{:S(2)}, u32[]{:S(2)}) collective-permute-start(f32[136,128]{1,0:T(8,128)S(1)} %get-tuple-element.64), channel_id=1, source_target_pairs={{0,1},{1,2},{2,3},{3,0},{4,5},{5,6},{6,7},{7,4},{8,9},{9,10},{10,1... | collective-permute-start | bytes 208904 | tf_op jit(solution)/shard_map/ppermute | solution.py:355
  6.3 11.9 %copy-start.1 = (f32[4352]{0:T(1024)S(1)}, f32[4352]{0:T(1024)}, u32[]{:S(2)}) copy-start(f32[4352]{0:T(1024)} %param.16) | copy-start | bytes 52228
  6.3 11.9 %copy-start.2 = (f32[1152]{0:T(1024)S(1)}, f32[1152]{0:T(1024)}, u32[]{:S(2)}) copy-start(f32[1152]{0:T(1024)} %param.17) | copy-start | bytes 13828
  8.2 20.8 %all-to-all-start = ((f32[128,1,384]{2,1,0:T(1,128)}), f32[128,1,384]{2,1,0:T(1,128)S(1)}, u32[]{:S(2)}, u32[]{:S(2)}) async-start(f32[128,1,384]{2,1,0:T(1,128)} %copy.45), calls=%async_computation | async-start | bytes 393216 | tf_op jit(solution)/shard_map/all_to_all | solution.py:452
  30.3 37.7 %collective-permute-start.2 = (f32[64,2432]{1,0:T(8,128)S(1)}, f32[64,2432]{1,0:T(8,128)S(1)}, u32[]{:S(2)}, u32[]{:S(2)}) collective-permute-start(f32[64,2432]{1,0:T(8,128)S(1)} %row_edges.2), channel_id=1, source_target_pairs={{4,0},{8,4},{12,8},{16,12},{20,16},{24,20},{28,24},{32,28},{36,32}... | collective-permute-start | bytes 1867784 | tf_op jit(solution)/shard_map/ppermute | solution.py:361
  40.4 27.6 %collective-permute-start.3 = (f32[64,2432]{1,0:T(8,128)S(1)}, f32[64,2432]{1,0:T(8,128)S(1)}, u32[]{:S(2)}, u32[]{:S(2)}) collective-permute-start(f32[64,2432]{1,0:T(8,128)S(1)} %row_edges.3), channel_id=1, source_target_pairs={{0,4},{4,8},{8,12},{12,16},{16,20},{20,24},{24,28},{28,32},{32,36}... | collective-permute-start | bytes 1867784 | tf_op jit(solution)/shard_map/ppermute | solution.py:361

commit v3 on v2

--- a/solution.py
+++ b/solution.py
@@ -196,17 +196,10 @@
         fourier_sums(rows, read, table_ref, out_ref, line_ref)
 
 
-def legendre_kernel(band, first, got_ref, legendre_ref, weight_ref, love_ref, *refs):
-    if first:
-        out_ref, held_ref, tiles_ref, line_ref, copies = refs
-    else:
-        out_ref, tiles_ref, line_ref = refs
-        held_ref = legendre_ref
+def table_kernel(legendre_ref, unused_ref, held_ref, turned_ref, copies):
     total, degrees = legendre_ref.shape
-    bands = total // band
-    count = total // LANES
     chunk = 2 * LANES
-    step = band - LANES
+    ahead = 4
 
     def copy(start):
         block = pl.ds(start, chunk)
@@ -214,9 +207,22 @@
             legendre_ref.at[block, :], held_ref.at[block, :], copies.at[start // chunk]
         )
 
-    if first:
-        for start in range(0, total, chunk):
-            copy(start).start()
+    for start in range(0, ahead * chunk, chunk):
+        copy(start).start()
+    for start in range(0, total, chunk):
+        copy(start).wait()
+        if start + ahead * chunk < total:
+            copy(start + ahead * chunk).start()
+        turned_ref[:, start : start + chunk] = jnp.transpose(held_ref[start : start + chunk, :])
+
+
+def legendre_kernel(
+    band, got_ref, legendre_ref, weight_ref, love_ref, turned_ref, out_ref, tiles_ref, line_ref
+):
+    total, degrees = legendre_ref.shape
+    bands = total // band
+    chunk = 2 * LANES
+    step = band - LANES
 
     message = received(got_ref, line_ref)
     tall = tiles_ref.shape[0] // 2
@@ -241,23 +247,21 @@
         weighted = jnp.concatenate(
             [tiles_ref[pl.ds(tile + i, 2, stride=tall), :] for i in range(2)], axis=1
         ).astype(LOW)
-        if first:
-            copy(start).wait()
         coeff = coeff + jnp.dot(
-            weighted, held_ref[start : start + chunk, :], preferred_element_type=HIGH
-        )
-    scaled = (coeff * love_ref[...]).astype(LOW)
+            weighted, legendre_ref[start : start + chunk, :], preferred_element_type=HIGH
+        )
+    coeff = jnp.concatenate([coeff * love_ref[...], jnp.zeros((6, degrees), HIGH)], axis=0)
+    scaled = coeff.astype(LOW)
     tiles_ref[...] = jnp.zeros_like(tiles_ref)
     for start in range(0, total, chunk):
-        back = lax.dot_general(
-            scaled,
-            held_ref[start : start + chunk, :],
-            (((1,), (1,)), ((), ())),
-            preferred_element_type=HIGH,
+        back = jnp.dot(
+            scaled, turned_ref[:, start : start + chunk], preferred_element_type=HIGH
         )
         row = tall - 2 - start // LANES
         for i in range(2):
-            tiles_ref[pl.ds(row - i, 2, stride=tall), :] = back[:, i * LANES : (i + 1) * LANES]
+            for k in range(2):
+                at = k * tall + row - i
+                tiles_ref[at : at + 1, :] = back[k : k + 1, i * LANES : (i + 1) * LANES]
     parts = []
     reach = LANES - HALO + step * (bands - 1 - rows_of((bands, LANES)))
     for k in range(2):
@@ -327,7 +331,7 @@
         pltpu.make_async_copy(field, target, copies.at[index])
         for index, (field, target) in enumerate(zip(fields, targets))
     ]
-    for move in moves[::-1]:
+    for move in moves[4:] + moves[:4]:
         move.start()
     for index, out in enumerate(outs):
         out[:rows, cols:] = ghost_tile(index, from_east[...], from_west[...])
@@ -451,28 +455,27 @@
         first, last = step == 0, step == STEPS - 1
         spectral = lax.all_to_all(sums, BOTH, split_axis=0, concat_axis=0, tiled=True)
         if first:
-            back, legendre = pl.pallas_call(
-                lambda *refs: legendre_kernel(rows, True, *refs),
-                out_shape=(message, pltpu.VMEM(legendre.shape, LOW)),
-                in_specs=[VMEM, pl.BlockSpec(memory_space=pl.ANY), VMEM, VMEM],
+            from_north = shifted_open(row_edge(0, 0, spectral), "lat", -1)
+            legendre, turned = pl.pallas_call(
+                table_kernel,
+                out_shape=(pltpu.VMEM(legendre.shape, LOW), pltpu.VMEM(legendre.shape[::-1], LOW)),
+                in_specs=[pl.BlockSpec(memory_space=pl.ANY)] * 2,
                 out_specs=(VMEM,) * 2,
-                scratch_shapes=[tiles, line, pltpu.SemaphoreType.DMA((total_rows // 256,))],
+                scratch_shapes=[pltpu.SemaphoreType.DMA((total_rows // 256,))],
                 compiler_params=small,
-                name="legendre_first",
-            )(spectral, in_hbm(legendre), weight, love)
-        else:
-            back = pl.pallas_call(
-                lambda *refs: legendre_kernel(rows, False, *refs),
-                out_shape=message,
-                in_specs=[VMEM] * 4,
-                out_specs=VMEM,
-                scratch_shapes=[tiles, line],
-                compiler_params=small,
-                name="legendre_pair",
-            )(spectral, in_vmem(legendre), in_vmem(weight), in_vmem(love))
+                name="tables",
+            )(in_hbm(legendre), spectral)
+            from_south = shifted_open(row_edge(rows - 16, 16 - HALO, turned), "lat", 1)
+        back = pl.pallas_call(
+            lambda *refs: legendre_kernel(rows, *refs),
+            out_shape=message,
+            in_specs=[VMEM] * 5,
+            out_specs=VMEM,
+            scratch_shapes=[tiles, line],
+            compiler_params=small,
+            name="legendre_pair",
+        )(spectral, *[in_vmem(x) for x in (legendre, weight, love, turned)])
         if first:
-            from_north = shifted_open(row_edge(0, 0, spectral), "lat", -1)
-            from_south = shifted_open(row_edge(rows - 16, 16 - HALO, back), "lat", 1)
             level, east, north, bathy, wet, east_open, north_open = pl.pallas_call(
                 assemble_kernel,
                 out_shape=(held,) * 7,

time: 503 us -> 486 us (0.966)
  Pallas kernels: 109 us -> 95.5 us
    pallas_call x12 -> x13, Pallas kernels: 55.6 us -> 44.7 us  [the longest x12 38.5 us: shards(): pl.pallas_call(lambda *refs: legendre_kernel(rows, *refs), out_shape=mess...]
where the time goes in v3:
time: 486 us; the launch traced here: 477 us
  blocking collectives  344 us (71%)
  Pallas kernels  95.5 us (20%)
  starting transfers between devices  18.1 us (4%)
  waiting for transfers between devices  10.7 us (2%)
  local copies, waits for them, and re-layouts  5.94 us (1%)
    all_to_all x12, blocking collectives, shards(): bands = lax.all_to_all(back, BOTH, split_axis=0, concat_axis=0, tiled=True)  182 us
    all_to_all x11, blocking collectives, shards(): lax.all_to_all(sums, BOTH, split_axis=0, concat_axis=0, tiled=True)  162 us
    pallas_call x11, Pallas kernels, shards(): pl.pallas_call(lambda *refs: grid_kernel(padded_rows, False, *refs), out_...  38.6 us
    pallas_call x12, Pallas kernels, shards(): pl.pallas_call(lambda *refs: legendre_kernel(rows, *refs), out_shape=mess...  38.5 us
    all_to_all x1, waiting for transfers between devices, shards(): lax.all_to_all(sums, BOTH, split_axis=0, concat_axis=0, tiled=True)  10.7 us
    all_to_all x1, starting transfers between devices, shards(): lax.all_to_all(sums, BOTH, split_axis=0, concat_axis=0, tiled=True)  10 us
  transfers between devices with their start and end apart: 5, of which 1 were waited for; matrix products, arithmetic and copies ran while one was open for 1% of the time, Pallas kernels for 2%

profile of v3, /device:TPU:1, one launch (start us, length us, event | category | flops | bytes accessed | tf_op | source)
XLA Modules:
  0.0 477.4 jit_solution(2017464515365383315)
XLA Ops:
  18.2 10.7 %all-to-all-done = f32[128,1,384]{2,1,0:T(1,128)S(1)} async-done(((f32[128,1,384]{2,1,0:T(1,128)}), f32[128,1,384]{2,1,0:T(1,128)S(1)}, u32[]{:S(2)}, u32[]{:S(2)}) %all-to-all-start) | async-done | bytes 196640 | tf_op jit(solution)/shard_map/all_to_all | solution.py:456
  46.6 20.0 %all_to_all.264 = f32[128,1,384]{2,1,0:T(1,128)S(1)} all-to-all(f32[128,1,384]{2,1,0:T(1,128)S(1)} %copy.46), channel_id=1, replica_groups=mesh['lat'=32,'lon'=4] {'lat','lon'}, dimensions={0} | all-to-all | bytes 393216 | tf_op jit(solution)/shard_map/all_to_all | solution.py:488
  73.2 15.5 %all_to_all.265 = f32[128,1,384]{2,1,0:T(1,128)S(1)} all-to-all(f32[128,1,384]{2,1,0:T(1,128)S(1)} %copy.47), channel_id=1, replica_groups=mesh['lat'=32,'lon'=4] {'lat','lon'}, dimensions={0} | all-to-all | bytes 393216 | tf_op jit(solution)/shard_map/all_to_all | solution.py:456
  92.2 14.6 %all_to_all.266 = f32[128,1,384]{2,1,0:T(1,128)S(1)} all-to-all(f32[128,1,384]{2,1,0:T(1,128)S(1)} %copy.48), channel_id=1, replica_groups=mesh['lat'=32,'lon'=4] {'lat','lon'}, dimensions={0} | all-to-all | bytes 393216 | tf_op jit(solution)/shard_map/all_to_all | solution.py:488
  110.5 14.6 %all_to_all.267 = f32[128,1,384]{2,1,0:T(1,128)S(1)} all-to-all(f32[128,1,384]{2,1,0:T(1,128)S(1)} %copy.49), channel_id=1, replica_groups=mesh['lat'=32,'lon'=4] {'lat','lon'}, dimensions={0} | all-to-all | bytes 393216 | tf_op jit(solution)/shard_map/all_to_all | solution.py:456
  128.5 14.6 %all_to_all.268 = f32[128,1,384]{2,1,0:T(1,128)S(1)} all-to-all(f32[128,1,384]{2,1,0:T(1,128)S(1)} %copy.50), channel_id=1, replica_groups=mesh['lat'=32,'lon'=4] {'lat','lon'}, dimensions={0} | all-to-all | bytes 393216 | tf_op jit(solution)/shard_map/all_to_all | solution.py:488
  146.9 14.6 %all_to_all.269 = f32[128,1,384]{2,1,0:T(1,128)S(1)} all-to-all(f32[128,1,384]{2,1,0:T(1,128)S(1)} %copy.51), channel_id=1, replica_groups=mesh['lat'=32,'lon'=4] {'lat','lon'}, dimensions={0} | all-to-all | bytes 393216 | tf_op jit(solution)/shard_map/all_to_all | solution.py:456
  164.9 14.8 %all_to_all.270 = f32[128,1,384]{2,1,0:T(1,128)S(1)} all-to-all(f32[128,1,384]{2,1,0:T(1,128)S(1)} %copy.52), channel_id=1, replica_groups=mesh['lat'=32,'lon'=4] {'lat','lon'}, dimensions={0} | all-to-all | bytes 393216 | tf_op jit(solution)/shard_map/all_to_all | solution.py:488
  183.5 14.6 %all_to_all.271 = f32[128,1,384]{2,1,0:T(1,128)S(1)} all-to-all(f32[128,1,384]{2,1,0:T(1,128)S(1)} %copy.53), channel_id=1, replica_groups=mesh['lat'=32,'lon'=4] {'lat','lon'}, dimensions={0} | all-to-all | bytes 393216 | tf_op jit(solution)/shard_map/all_to_all | solution.py:456
  201.6 14.6 %all_to_all.272 = f32[128,1,384]{2,1,0:T(1,128)S(1)} all-to-all(f32[128,1,384]{2,1,0:T(1,128)S(1)} %copy.54), channel_id=1, replica_groups=mesh['lat'=32,'lon'=4] {'lat','lon'}, dimensions={0} | all-to-all | bytes 393216 | tf_op jit(solution)/shard_map/all_to_all | solution.py:488
  219.9 14.9 %all_to_all.273 = f32[128,1,384]{2,1,0:T(1,128)S(1)} all-to-all(f32[128,1,384]{2,1,0:T(1,128)S(1)} %copy.55), channel_id=1, replica_groups=mesh['lat'=32,'lon'=4] {'lat','lon'}, dimensions={0} | all-to-all | bytes 393216 | tf_op jit(solution)/shard_map/all_to_all | solution.py:456
  238.2 14.6 %all_to_all.274 = f32[128,1,384]{2,1,0:T(1,128)S(1)} all-to-all(f32[128,1,384]{2,1,0:T(1,128)S(1)} %copy.56), channel_id=1, replica_groups=mesh['lat'=32,'lon'=4] {'lat','lon'}, dimensions={0} | all-to-all | bytes 393216 | tf_op jit(solution)/shard_map/all_to_all | solution.py:488
  256.6 14.6 %all_to_all.275 = f32[128,1,384]{2,1,0:T(1,128)S(1)} all-to-all(f32[128,1,384]{2,1,0:T(1,128)S(1)} %copy.57), channel_id=1, replica_groups=mesh['lat'=32,'lon'=4] {'lat','lon'}, dimensions={0} | all-to-all | bytes 393216 | tf_op jit(solution)/shard_map/all_to_all | solution.py:456
  274.7 15.1 %all_to_all.276 = f32[128,1,384]{2,1,0:T(1,128)S(1)} all-to-all(f32[128,1,384]{2,1,0:T(1,128)S(1)} %copy.58), channel_id=1, replica_groups=mesh['lat'=32,'lon'=4] {'lat','lon'}, dimensions={0} | all-to-all | bytes 393216 | tf_op jit(solution)/shard_map/all_to_all | solution.py:488
  293.5 14.6 %all_to_all.277 = f32[128,1,384]{2,1,0:T(1,128)S(1)} all-to-all(f32[128,1,384]{2,1,0:T(1,128)S(1)} %copy.59), channel_id=1, replica_groups=mesh['lat'=32,'lon'=4] {'lat','lon'}, dimensions={0} | all-to-all | bytes 393216 | tf_op jit(solution)/shard_map/all_to_all | solution.py:456
  311.6 14.6 %all_to_all.278 = f32[128,1,384]{2,1,0:T(1,128)S(1)} all-to-all(f32[128,1,384]{2,1,0:T(1,128)S(1)} %copy.60), channel_id=1, replica_groups=mesh['lat'=32,'lon'=4] {'lat','lon'}, dimensions={0} | all-to-all | bytes 393216 | tf_op jit(solution)/shard_map/all_to_all | solution.py:488
  329.9 14.8 %all_to_all.279 = f32[128,1,384]{2,1,0:T(1,128)S(1)} all-to-all(f32[128,1,384]{2,1,0:T(1,128)S(1)} %copy.61), channel_id=1, replica_groups=mesh['lat'=32,'lon'=4] {'lat','lon'}, dimensions={0} | all-to-all | bytes 393216 | tf_op jit(solution)/shard_map/all_to_all | solution.py:456
  348.2 14.6 %all_to_all.280 = f32[128,1,384]{2,1,0:T(1,128)S(1)} all-to-all(f32[128,1,384]{2,1,0:T(1,128)S(1)} %copy.62), channel_id=1, replica_groups=mesh['lat'=32,'lon'=4] {'lat','lon'}, dimensions={0} | all-to-all | bytes 393216 | tf_op jit(solution)/shard_map/all_to_all | solution.py:488
  366.6 14.6 %all_to_all.281 = f32[128,1,384]{2,1,0:T(1,128)S(1)} all-to-all(f32[128,1,384]{2,1,0:T(1,128)S(1)} %copy.63), channel_id=1, replica_groups=mesh['lat'=32,'lon'=4] {'lat','lon'}, dimensions={0} | all-to-all | bytes 393216 | tf_op jit(solution)/shard_map/all_to_all | solution.py:456
  384.6 14.9 %all_to_all.282 = f32[128,1,384]{2,1,0:T(1,128)S(1)} all-to-all(f32[128,1,384]{2,1,0:T(1,128)S(1)} %copy.64), channel_id=1, replica_groups=mesh['lat'=32,'lon'=4] {'lat','lon'}, dimensions={0} | all-to-all | bytes 393216 | tf_op jit(solution)/shard_map/all_to_all | solution.py:488
  403.2 14.6 %all_to_all.283 = f32[128,1,384]{2,1,0:T(1,128)S(1)} all-to-all(f32[128,1,384]{2,1,0:T(1,128)S(1)} %copy.65), channel_id=1, replica_groups=mesh['lat'=32,'lon'=4] {'lat','lon'}, dimensions={0} | all-to-all | bytes 393216 | tf_op jit(solution)/shard_map/all_to_all | solution.py:456
  421.3 14.6 %all_to_all.284 = f32[128,1,384]{2,1,0:T(1,128)S(1)} all-to-all(f32[128,1,384]{2,1,0:T(1,128)S(1)} %copy.66), channel_id=1, replica_groups=mesh['lat'=32,'lon'=4] {'lat','lon'}, dimensions={0} | all-to-all | bytes 393216 | tf_op jit(solution)/shard_map/all_to_all | solution.py:488
  439.6 14.9 %all_to_all.285 = f32[128,1,384]{2,1,0:T(1,128)S(1)} all-to-all(f32[128,1,384]{2,1,0:T(1,128)S(1)} %copy.67), channel_id=1, replica_groups=mesh['lat'=32,'lon'=4] {'lat','lon'}, dimensions={0} | all-to-all | bytes 393216 | tf_op jit(solution)/shard_map/all_to_all | solution.py:456
  458.0 14.6 %all_to_all.286 = f32[128,1,384]{2,1,0:T(1,128)S(1)} all-to-all(f32[128,1,384]{2,1,0:T(1,128)S(1)} %copy.68), channel_id=1, replica_groups=mesh['lat'=32,'lon'=4] {'lat','lon'}, dimensions={0} | all-to-all | bytes 393216 | tf_op jit(solution)/shard_map/all_to_all | solution.py:488
  (103 shorter events, 120.9 us)
Async XLA Ops:
  0.6 4.2 copy-start.3
  2.1 4.2 copy-start
  2.1 16.1 %collective-permute-start = (f32[136,128]{1,0:T(8,128)S(1)}, f32[136,128]{1,0:T(8,128)S(1)}, u32[]{:S(2)}, u32[]{:S(2)}) collective-permute-start(f32[136,128]{1,0:T(8,128)S(1)} %get-tuple-element.64), channel_id=1, source_target_pairs={{0,3},{1,0},{2,1},{3,2},{4,7},{5,4},{6,5},{7,6},{8,11},{9,8},{10,9... | collective-permute-start | bytes 208904 | tf_op jit(solution)/shard_map/ppermute | solution.py:359
  3.6 14.6 %collective-permute-start.1 = (f32[136,128]{1,0:T(8,128)S(1)}, f32[136,128]{1,0:T(8,128)S(1)}, u32[]{:S(2)}, u32[]{:S(2)}) collective-permute-start(f32[136,128]{1,0:T(8,128)S(1)} %get-tuple-element.65), channel_id=1, source_target_pairs={{0,1},{1,2},{2,3},{3,0},{4,5},{5,6},{6,7},{7,4},{8,9},{9,10},{10,1... | collective-permute-start | bytes 208904 | tf_op jit(solution)/shard_map/ppermute | solution.py:359
  8.1 20.8 %all-to-all-start = ((f32[128,1,384]{2,1,0:T(1,128)}), f32[128,1,384]{2,1,0:T(1,128)S(1)}, u32[]{:S(2)}, u32[]{:S(2)}) async-start(f32[128,1,384]{2,1,0:T(1,128)} %copy.45), calls=%async_computation | async-start | bytes 393216 | tf_op jit(solution)/shard_map/all_to_all | solution.py:456
  30.2 36.4 %collective-permute-start.2 = (f32[64,2432]{1,0:T(8,128)S(1)}, f32[64,2432]{1,0:T(8,128)S(1)}, u32[]{:S(2)}, u32[]{:S(2)}) collective-permute-start(f32[64,2432]{1,0:T(8,128)S(1)} %row_edges.2), channel_id=1, source_target_pairs={{4,0},{8,4},{12,8},{16,12},{20,16},{24,20},{28,24},{32,28},{36,32}... | collective-permute-start | bytes 1867784 | tf_op jit(solution)/shard_map/ppermute | solution.py:365
  37.7 5.4 %copy-start.2 = (f32[1152]{0:T(1024)S(1)}, f32[1152]{0:T(1024)}, u32[]{:S(2)}) copy-start(f32[1152]{0:T(1024)} %param.17) | copy-start | bytes 13828
  37.8 5.4 %copy-start.1 = (f32[4352]{0:T(1024)S(1)}, f32[4352]{0:T(1024)}, u32[]{:S(2)}) copy-start(f32[4352]{0:T(1024)} %param.16) | copy-start | bytes 52228
  39.1 27.5 %collective-permute-start.3 = (f32[64,2432]{1,0:T(8,128)S(1)}, f32[64,2432]{1,0:T(8,128)S(1)}, u32[]{:S(2)}, u32[]{:S(2)}) collective-permute-start(f32[64,2432]{1,0:T(8,128)S(1)} %row_edges.3), channel_id=1, source_target_pairs={{0,4},{4,8},{8,12},{12,16},{16,20},{20,24},{24,28},{28,32},{32,36}... | collective-permute-start | bytes 1867784 | tf_op jit(solution)/shard_map/ppermute | solution.py:365

commit v4 on v3

--- a/solution.py
+++ b/solution.py
@@ -199,7 +199,7 @@
 def table_kernel(legendre_ref, unused_ref, held_ref, turned_ref, copies):
     total, degrees = legendre_ref.shape
     chunk = 2 * LANES
-    ahead = 4
+    ahead = 8
 
     def copy(start):
         block = pl.ds(start, chunk)
@@ -449,13 +449,14 @@
         name="first_sums",
     )(height, basis)
 
+    from_north = shifted_open(row_edge(0, 0, sums), "lat", -1)
     held = pltpu.VMEM((tall, wide), HIGH)
     tiles = pltpu.VMEM((80, LANES), HIGH)
     for step in range(STEPS):
         first, last = step == 0, step == STEPS - 1
         spectral = lax.all_to_all(sums, BOTH, split_axis=0, concat_axis=0, tiled=True)
         if first:
-            from_north = shifted_open(row_edge(0, 0, spectral), "lat", -1)
+            from_south = shifted_open(row_edge(rows - 16, 16 - HALO, spectral), "lat", 1)
             legendre, turned = pl.pallas_call(
                 table_kernel,
                 out_shape=(pltpu.VMEM(legendre.shape, LOW), pltpu.VMEM(legendre.shape[::-1], LOW)),
@@ -465,7 +466,6 @@
                 compiler_params=small,
                 name="tables",
             )(in_hbm(legendre), spectral)
-            from_south = shifted_open(row_edge(rows - 16, 16 - HALO, turned), "lat", 1)
         back = pl.pallas_call(
             lambda *refs: legendre_kernel(rows, *refs),
             out_shape=message,

time: 486 us -> 480 us (0.988)
  no operation moved by 1% of the time
where the time goes in v4:
time: 480 us; the launch traced here: 471 us
  blocking collectives  342 us (71%)
  Pallas kernels  95.8 us (20%)
  starting transfers between devices  16.2 us (3%)
  waiting for transfers between devices  8.08 us (2%)
  local copies, waits for them, and re-layouts  5.93 us (1%)
    all_to_all x12, blocking collectives, shards(): bands = lax.all_to_all(back, BOTH, split_axis=0, concat_axis=0, tiled=True)  181 us
    all_to_all x11, blocking collectives, shards(): lax.all_to_all(sums, BOTH, split_axis=0, concat_axis=0, tiled=True)  162 us
    pallas_call x11, Pallas kernels, shards(): pl.pallas_call(lambda *refs: grid_kernel(padded_rows, False, *refs), out_...  38.6 us
    pallas_call x12, Pallas kernels, shards(): pl.pallas_call(lambda *refs: legendre_kernel(rows, *refs), out_shape=mess...  38.5 us
    all_to_all x1, starting transfers between devices, shards(): lax.all_to_all(sums, BOTH, split_axis=0, concat_axis=0, tiled=True)  10 us
  transfers between devices with their start and end apart: 5, of which 1 were waited for; matrix products, arithmetic and copies ran while one was open for 1% of the time, Pallas kernels for 2%

profile of v4, /device:TPU:1, one launch (start us, length us, event | category | flops | bytes accessed | tf_op | source)
XLA Modules:
  0.0 471.4 jit_solution(1570122184392499318)
XLA Ops:
  8.6 10.0 %all-to-all-start = ((f32[128,1,384]{2,1,0:T(1,128)}), f32[128,1,384]{2,1,0:T(1,128)S(1)}, u32[]{:S(2)}, u32[]{:S(2)}) async-start(f32[128,1,384]{2,1,0:T(1,128)} %copy.45), calls=%async_computation | async-start | bytes 393216 | tf_op jit(solution)/shard_map/all_to_all | solution.py:457
  41.3 19.1 %all_to_all.264 = f32[128,1,384]{2,1,0:T(1,128)S(1)} all-to-all(f32[128,1,384]{2,1,0:T(1,128)S(1)} %copy.46), channel_id=1, replica_groups=mesh['lat'=32,'lon'=4] {'lat','lon'}, dimensions={0} | all-to-all | bytes 393216 | tf_op jit(solution)/shard_map/all_to_all | solution.py:488
  68.2 14.6 %all_to_all.265 = f32[128,1,384]{2,1,0:T(1,128)S(1)} all-to-all(f32[128,1,384]{2,1,0:T(1,128)S(1)} %copy.47), channel_id=1, replica_groups=mesh['lat'=32,'lon'=4] {'lat','lon'}, dimensions={0} | all-to-all | bytes 393216 | tf_op jit(solution)/shard_map/all_to_all | solution.py:457
  86.2 14.6 %all_to_all.266 = f32[128,1,384]{2,1,0:T(1,128)S(1)} all-to-all(f32[128,1,384]{2,1,0:T(1,128)S(1)} %copy.48), channel_id=1, replica_groups=mesh['lat'=32,'lon'=4] {'lat','lon'}, dimensions={0} | all-to-all | bytes 393216 | tf_op jit(solution)/shard_map/all_to_all | solution.py:488
  104.6 14.6 %all_to_all.267 = f32[128,1,384]{2,1,0:T(1,128)S(1)} all-to-all(f32[128,1,384]{2,1,0:T(1,128)S(1)} %copy.49), channel_id=1, replica_groups=mesh['lat'=32,'lon'=4] {'lat','lon'}, dimensions={0} | all-to-all | bytes 393216 | tf_op jit(solution)/shard_map/all_to_all | solution.py:457
  122.6 14.6 %all_to_all.268 = f32[128,1,384]{2,1,0:T(1,128)S(1)} all-to-all(f32[128,1,384]{2,1,0:T(1,128)S(1)} %copy.50), channel_id=1, replica_groups=mesh['lat'=32,'lon'=4] {'lat','lon'}, dimensions={0} | all-to-all | bytes 393216 | tf_op jit(solution)/shard_map/all_to_all | solution.py:488
  140.9 14.6 %all_to_all.269 = f32[128,1,384]{2,1,0:T(1,128)S(1)} all-to-all(f32[128,1,384]{2,1,0:T(1,128)S(1)} %copy.51), channel_id=1, replica_groups=mesh['lat'=32,'lon'=4] {'lat','lon'}, dimensions={0} | all-to-all | bytes 393216 | tf_op jit(solution)/shard_map/all_to_all | solution.py:457
  159.0 14.8 %all_to_all.270 = f32[128,1,384]{2,1,0:T(1,128)S(1)} all-to-all(f32[128,1,384]{2,1,0:T(1,128)S(1)} %copy.52), channel_id=1, replica_groups=mesh['lat'=32,'lon'=4] {'lat','lon'}, dimensions={0} | all-to-all | bytes 393216 | tf_op jit(solution)/shard_map/all_to_all | solution.py:488
  177.6 14.6 %all_to_all.271 = f32[128,1,384]{2,1,0:T(1,128)S(1)} all-to-all(f32[128,1,384]{2,1,0:T(1,128)S(1)} %copy.53), channel_id=1, replica_groups=mesh['lat'=32,'lon'=4] {'lat','lon'}, dimensions={0} | all-to-all | bytes 393216 | tf_op jit(solution)/shard_map/all_to_all | solution.py:457
  195.6 14.6 %all_to_all.272 = f32[128,1,384]{2,1,0:T(1,128)S(1)} all-to-all(f32[128,1,384]{2,1,0:T(1,128)S(1)} %copy.54), channel_id=1, replica_groups=mesh['lat'=32,'lon'=4] {'lat','lon'}, dimensions={0} | all-to-all | bytes 393216 | tf_op jit(solution)/shard_map/all_to_all | solution.py:488
  214.0 14.9 %all_to_all.273 = f32[128,1,384]{2,1,0:T(1,128)S(1)} all-to-all(f32[128,1,384]{2,1,0:T(1,128)S(1)} %copy.55), channel_id=1, replica_groups=mesh['lat'=32,'lon'=4] {'lat','lon'}, dimensions={0} | all-to-all | bytes 393216 | tf_op jit(solution)/shard_map/all_to_all | solution.py:457
  232.3 14.6 %all_to_all.274 = f32[128,1,384]{2,1,0:T(1,128)S(1)} all-to-all(f32[128,1,384]{2,1,0:T(1,128)S(1)} %copy.56), channel_id=1, replica_groups=mesh['lat'=32,'lon'=4] {'lat','lon'}, dimensions={0} | all-to-all | bytes 393216 | tf_op jit(solution)/shard_map/all_to_all | solution.py:488
  250.7 14.6 %all_to_all.275 = f32[128,1,384]{2,1,0:T(1,128)S(1)} all-to-all(f32[128,1,384]{2,1,0:T(1,128)S(1)} %copy.57), channel_id=1, replica_groups=mesh['lat'=32,'lon'=4] {'lat','lon'}, dimensions={0} | all-to-all | bytes 393216 | tf_op jit(solution)/shard_map/all_to_all | solution.py:457
  268.7 15.1 %all_to_all.276 = f32[128,1,384]{2,1,0:T(1,128)S(1)} all-to-all(f32[128,1,384]{2,1,0:T(1,128)S(1)} %copy.58), channel_id=1, replica_groups=mesh['lat'=32,'lon'=4] {'lat','lon'}, dimensions={0} | all-to-all | bytes 393216 | tf_op jit(solution)/shard_map/all_to_all | solution.py:488
  287.5 14.6 %all_to_all.277 = f32[128,1,384]{2,1,0:T(1,128)S(1)} all-to-all(f32[128,1,384]{2,1,0:T(1,128)S(1)} %copy.59), channel_id=1, replica_groups=mesh['lat'=32,'lon'=4] {'lat','lon'}, dimensions={0} | all-to-all | bytes 393216 | tf_op jit(solution)/shard_map/all_to_all | solution.py:457
  305.6 14.6 %all_to_all.278 = f32[128,1,384]{2,1,0:T(1,128)S(1)} all-to-all(f32[128,1,384]{2,1,0:T(1,128)S(1)} %copy.60), channel_id=1, replica_groups=mesh['lat'=32,'lon'=4] {'lat','lon'}, dimensions={0} | all-to-all | bytes 393216 | tf_op jit(solution)/shard_map/all_to_all | solution.py:488
  323.9 14.8 %all_to_all.279 = f32[128,1,384]{2,1,0:T(1,128)S(1)} all-to-all(f32[128,1,384]{2,1,0:T(1,128)S(1)} %copy.61), channel_id=1, replica_groups=mesh['lat'=32,'lon'=4] {'lat','lon'}, dimensions={0} | all-to-all | bytes 393216 | tf_op jit(solution)/shard_map/all_to_all | solution.py:457
  342.2 14.6 %all_to_all.280 = f32[128,1,384]{2,1,0:T(1,128)S(1)} all-to-all(f32[128,1,384]{2,1,0:T(1,128)S(1)} %copy.62), channel_id=1, replica_groups=mesh['lat'=32,'lon'=4] {'lat','lon'}, dimensions={0} | all-to-all | bytes 393216 | tf_op jit(solution)/shard_map/all_to_all | solution.py:488
  360.6 14.6 %all_to_all.281 = f32[128,1,384]{2,1,0:T(1,128)S(1)} all-to-all(f32[128,1,384]{2,1,0:T(1,128)S(1)} %copy.63), channel_id=1, replica_groups=mesh['lat'=32,'lon'=4] {'lat','lon'}, dimensions={0} | all-to-all | bytes 393216 | tf_op jit(solution)/shard_map/all_to_all | solution.py:457
  378.7 14.9 %all_to_all.282 = f32[128,1,384]{2,1,0:T(1,128)S(1)} all-to-all(f32[128,1,384]{2,1,0:T(1,128)S(1)} %copy.64), channel_id=1, replica_groups=mesh['lat'=32,'lon'=4] {'lat','lon'}, dimensions={0} | all-to-all | bytes 393216 | tf_op jit(solution)/shard_map/all_to_all | solution.py:488
  397.3 14.6 %all_to_all.283 = f32[128,1,384]{2,1,0:T(1,128)S(1)} all-to-all(f32[128,1,384]{2,1,0:T(1,128)S(1)} %copy.65), channel_id=1, replica_groups=mesh['lat'=32,'lon'=4] {'lat','lon'}, dimensions={0} | all-to-all | bytes 393216 | tf_op jit(solution)/shard_map/all_to_all | solution.py:457
  415.4 14.6 %all_to_all.284 = f32[128,1,384]{2,1,0:T(1,128)S(1)} all-to-all(f32[128,1,384]{2,1,0:T(1,128)S(1)} %copy.66), channel_id=1, replica_groups=mesh['lat'=32,'lon'=4] {'lat','lon'}, dimensions={0} | all-to-all | bytes 393216 | tf_op jit(solution)/shard_map/all_to_all | solution.py:488
  433.7 14.9 %all_to_all.285 = f32[128,1,384]{2,1,0:T(1,128)S(1)} all-to-all(f32[128,1,384]{2,1,0:T(1,128)S(1)} %copy.67), channel_id=1, replica_groups=mesh['lat'=32,'lon'=4] {'lat','lon'}, dimensions={0} | all-to-all | bytes 393216 | tf_op jit(solution)/shard_map/all_to_all | solution.py:457
  452.1 14.6 %all_to_all.286 = f32[128,1,384]{2,1,0:T(1,128)S(1)} all-to-all(f32[128,1,384]{2,1,0:T(1,128)S(1)} %copy.68), channel_id=1, replica_groups=mesh['lat'=32,'lon'=4] {'lat','lon'}, dimensions={0} | all-to-all | bytes 393216 | tf_op jit(solution)/shard_map/all_to_all | solution.py:488
  (103 shorter events, 117.4 us)
Async XLA Ops:
  0.6 4.8 %copy-start.3 = (s32[32]{0:T(128)S(1)}, s32[32]{0:T(128)}, u32[]{:S(2)}) copy-start(s32[32]{0:T(128)} %param.14) | copy-start | bytes 388
  2.7 4.1 copy-start
  2.7 16.0 %collective-permute-start = (f32[136,128]{1,0:T(8,128)}, f32[136,128]{1,0:T(8,128)S(1)}, u32[]{:S(2)}, u32[]{:S(2)}) collective-permute-start(f32[136,128]{1,0:T(8,128)} %get-tuple-element.64), channel_id=1, source_target_pairs={{0,3},{1,0},{2,1},{3,2},{4,7},{5,4},{6,5},{7,6},{8,11},{9,8},{10,9... | collective-permute-start | bytes 208904 | tf_op jit(solution)/shard_map/ppermute | solution.py:359
  4.1 14.6 %collective-permute-start.1 = (f32[136,128]{1,0:T(8,128)S(1)}, f32[136,128]{1,0:T(8,128)S(1)}, u32[]{:S(2)}, u32[]{:S(2)}) collective-permute-start(f32[136,128]{1,0:T(8,128)S(1)} %get-tuple-element.65), channel_id=1, source_target_pairs={{0,1},{1,2},{2,3},{3,0},{4,5},{5,6},{6,7},{7,4},{8,9},{9,10},{10,1... | collective-permute-start | bytes 208904 | tf_op jit(solution)/shard_map/ppermute | solution.py:359
  8.6 20.8 %all-to-all-start = ((f32[128,1,384]{2,1,0:T(1,128)}), f32[128,1,384]{2,1,0:T(1,128)S(1)}, u32[]{:S(2)}, u32[]{:S(2)}) async-start(f32[128,1,384]{2,1,0:T(1,128)} %copy.45), calls=%async_computation | async-start | bytes 393216 | tf_op jit(solution)/shard_map/all_to_all | solution.py:457
  20.0 40.4 %collective-permute-start.2 = (f32[64,2432]{1,0:T(8,128)S(1)}, f32[64,2432]{1,0:T(8,128)}, u32[]{:S(2)}, u32[]{:S(2)}) collective-permute-start(f32[64,2432]{1,0:T(8,128)S(1)} %row_edges.2), channel_id=1, source_target_pairs={{4,0},{8,4},{12,8},{16,12},{20,16},{24,20},{28,24},{32,28},{36,32}... | collective-permute-start | bytes 1867784 | tf_op jit(solution)/shard_map/ppermute | solution.py:365
  29.4 3.6 copy-start.2
  29.4 3.6 copy-start.1
  30.8 29.7 %collective-permute-start.3 = (f32[64,2432]{1,0:T(8,128)S(1)}, f32[64,2432]{1,0:T(8,128)S(1)}, u32[]{:S(2)}, u32[]{:S(2)}) collective-permute-start(f32[64,2432]{1,0:T(8,128)S(1)} %row_edges.3), channel_id=1, source_target_pairs={{0,4},{4,8},{8,12},{12,16},{16,20},{20,24},{24,28},{28,32},{32,36}... | collective-permute-start | bytes 1867784 | tf_op jit(solution)/shard_map/ppermute | solution.py:365

commit v5 on v4

--- a/solution.py
+++ b/solution.py
@@ -12,6 +12,7 @@
 LANES = 128
 SECOND = 192
 MSG = 384
+LEAVE = 24
 SLOT = 16
 
 gravity_step = 0.12
@@ -117,11 +118,12 @@
     return jnp.concatenate([ref[start + 1 : tall, :], ref[:1, :]], axis=0)
 
 
-def grid_kernel(rows, last, *refs):
+def grid_kernel(rows, last, near, *refs):
     (got_ref, level_in, east_in, north_in, bathy_ref, wet_ref, east_open_ref, north_open_ref) = refs[:8]
     synth_ref, refs = refs[8], refs[9:]
     if last:
-        level_ref, east_ref, north_ref, pot_ref, depth_ref, south_ref, line_ref = refs
+        results, refs = refs[:3], refs[3:]
+        level_ref, east_ref, north_ref, pot_ref, depth_ref, south_ref, line_ref, copies = refs
     else:
         table_ref, level_ref, east_ref, north_ref, out_ref = refs[:5]
         pot_ref, depth_ref, south_ref, line_ref = refs[5:]
@@ -176,12 +178,26 @@
     if last:
         update(tall - 8)
         south_ref[:8, :] = south_ref[tall : tall + 8, :]
+        moves = []
+        begin = 0
         for start in range(0, own, 8):
             update(start)
+            end = start + 8
+            if end - begin == LEAVE or end == own:
+                for index, held in enumerate((level_ref, east_ref, north_ref)):
+                    block = pl.ds(begin, end - begin)
+                    move = pltpu.make_async_copy(
+                        held.at[block, :], results[index].at[block, :], copies.at[len(moves)]
+                    )
+                    move.start()
+                    moves.append(move)
+                begin = end
+        for move in moves:
+            move.wait()
     else:
         seam = tall - 2 * HALO
-        south_ref[seam : seam + 8, :] = jnp.zeros((8, wide), HIGH)
-        for start in range(seam, tall, 8):
+        south_ref[seam : tall + 8, :] = jnp.zeros((tall + 8 - seam, wide), HIGH)
+        for start in (seam, tall - 8) if near else range(seam, tall, 8):
             update(start)
         south_ref[:8, :] = south_ref[tall : tall + 8, :]
         for start in range(0, seam, 8):
@@ -308,22 +324,31 @@
     east_ref[...] = east
 
 
-def row_edge_kernel(begin, *refs):
-    fields, (from_east, from_west, unused_ref, out_ref) = refs[:-4], refs[-4:]
+def row_edge_kernel(northern_ref, *refs):
+    fields, refs = refs[:-6], refs[-6:]
+    east_low, east_high, west_low, west_high, unused_ref, out_ref = refs
     cols = fields[0].shape[1]
-    keep = slice(begin, begin + HALO)
-    out_ref[len(fields) // 2 * HALO :, :] = jnp.zeros_like(out_ref[len(fields) // 2 * HALO :, :])
-    for index in range(len(fields) // 2):
-        both = jnp.concatenate([ref[...].astype(HIGH) for ref in fields[2 * index : 2 * index + 2]], axis=0)
+    northern = northern_ref[0] == 1
+
+    def keep(low, high):
+        both = jnp.concatenate([low, high], axis=0).astype(HIGH)
+        return jnp.where(northern, both[16 - HALO :], both[:HALO])
+
+    count = len(fields) // 2
+    out_ref[count * HALO :, :] = jnp.zeros_like(out_ref[count * HALO :, :])
+    from_east = keep(east_low[...], east_high[...])
+    from_west = keep(west_low[...], west_high[...])
+    for index in range(count):
         where = slice(HALO * index, HALO * (index + 1))
-        out_ref[where, :cols] = both[keep]
-        out_ref[where, cols:] = ghost_tile(index, from_east[...], from_west[...])[keep]
+        out_ref[where, :cols] = keep(fields[2 * index][...], fields[2 * index + 1][...])
+        out_ref[where, cols:] = ghost_tile(index, from_east, from_west)
 
 
 def assemble_kernel(*refs):
     fields, refs = refs[:5], refs[5:]
-    (from_east, from_west, from_north, from_south), refs = refs[:4], refs[4:]
+    (from_east, from_west, early_ref, late_ref, even_ref), refs = refs[:5], refs[5:]
     outs, (east_open_ref, north_open_ref, mask_ref, copies) = refs[:5], refs[5:]
+    even = even_ref[0] == 1
     rows, cols = fields[0].shape
     tall, wide = outs[0].shape
     targets = [out.at[:rows, :cols] for out in outs[:4]] + [mask_ref]
@@ -336,8 +361,9 @@
     for index, out in enumerate(outs):
         out[:rows, cols:] = ghost_tile(index, from_east[...], from_west[...])
         begin = HALO * index
+        early, late = early_ref[begin : begin + HALO, :], late_ref[begin : begin + HALO, :]
         out[rows:, :] = jnp.concatenate(
-            [from_north[begin : begin + HALO, :], from_south[begin : begin + HALO, :]], axis=0
+            [jnp.where(even, early, late), jnp.where(even, late, early)], axis=0
         )
     moves[4].wait()
     wet_ref = outs[4]
@@ -357,12 +383,6 @@
 def shifted(value, axis, by):
     count = lax.axis_size(axis)
     return lax.ppermute(value, axis, [(i, (i + by) % count) for i in range(count)])
-
-
-def shifted_open(value, axis, by):
-    count = lax.axis_size(axis)
-    pairs = [(i, i + by) for i in range(count) if 0 <= i + by < count]
-    return lax.ppermute(value, axis, pairs)
 
 
 def shards(
@@ -407,23 +427,39 @@
     from_east = shifted(west_edge, "lon", -1)
     from_west = shifted(east_edge, "lon", 1)
 
-    def row_edge(start, keep, after):
-        block = [pl.BlockSpec((8, cols), lambda i, at=start // 8 + n: (at, 0)) for n in range(2)]
-        ghost = pl.BlockSpec((16, LANES), lambda i: (0, 0))
+    even = (1 - lax.axis_index("lat") % 2).astype(jnp.int32).reshape(1)
+
+    def row_edge(northern, after):
+        def end(width, n):
+            return pl.BlockSpec((8, width), lambda i, flag: (flag[0] * (rows // 8 - 2) + n, 0))
+
         return pl.pallas_call(
-            lambda *refs: row_edge_kernel(keep, *refs),
-            grid=(1,),
+            row_edge_kernel,
+            grid_spec=pltpu.PrefetchScalarGridSpec(
+                num_scalar_prefetch=1,
+                grid=(1,),
+                in_specs=[end(cols, 0), end(cols, 1)] * 5
+                + [end(LANES, 0), end(LANES, 1)] * 2
+                + [pl.BlockSpec(memory_space=pl.ANY)],
+                out_specs=pl.BlockSpec((64, wide), lambda i, flag: (0, 0)),
+            ),
             out_shape=jax.ShapeDtypeStruct((64, wide), HIGH),
-            in_specs=block * 5 + [ghost, ghost, pl.BlockSpec(memory_space=pl.ANY)],
-            out_specs=pl.BlockSpec((64, wide), lambda i: (0, 0)),
             compiler_params=small,
             name="row_edges",
         )(
+            northern,
             *[in_hbm(f) for f in fields for _ in range(2)],
-            from_east[start : start + 16],
-            from_west[start : start + 16],
+            from_east,
+            from_east,
+            from_west,
+            from_west,
             after,
         )
+
+    def swapped(value, begin):
+        count = lat_count
+        pairs = [(i, i + 1) for i in range(begin, count - 1, 2)]
+        return lax.ppermute(value, "lat", pairs + [(j, i) for i, j in pairs])
 
     lane = jnp.arange(wide, dtype=jnp.int32)
     offset = jnp.where(lane < cols + LANES // 2, lane, lane - wide)
@@ -449,14 +485,14 @@
         name="first_sums",
     )(height, basis)
 
-    from_north = shifted_open(row_edge(0, 0, sums), "lat", -1)
+    early = swapped(row_edge(even, sums), 0)
     held = pltpu.VMEM((tall, wide), HIGH)
     tiles = pltpu.VMEM((80, LANES), HIGH)
     for step in range(STEPS):
         first, last = step == 0, step == STEPS - 1
         spectral = lax.all_to_all(sums, BOTH, split_axis=0, concat_axis=0, tiled=True)
         if first:
-            from_south = shifted_open(row_edge(rows - 16, 16 - HALO, spectral), "lat", 1)
+            late = swapped(row_edge(1 - even, spectral), 1)
             legendre, turned = pl.pallas_call(
                 table_kernel,
                 out_shape=(pltpu.VMEM(legendre.shape, LOW), pltpu.VMEM(legendre.shape[::-1], LOW)),
@@ -479,12 +515,14 @@
             level, east, north, bathy, wet, east_open, north_open = pl.pallas_call(
                 assemble_kernel,
                 out_shape=(held,) * 7,
-                in_specs=[pl.BlockSpec(memory_space=pl.ANY)] * 5 + [VMEM] * 4,
+                in_specs=[pl.BlockSpec(memory_space=pl.ANY)] * 5
+                + [VMEM] * 4
+                + [pl.BlockSpec(memory_space=pltpu.SMEM)],
                 out_specs=(VMEM,) * 7,
                 scratch_shapes=[pltpu.VMEM((rows, cols), jnp.int32), pltpu.SemaphoreType.DMA((5,))],
                 compiler_params=small,
                 name="assemble",
-            )(*[in_hbm(f) for f in fields], from_east, from_west, from_north, from_south)
+            )(*[in_hbm(f) for f in fields], from_east, from_west, early, late, even)
         bands = lax.all_to_all(back, BOTH, split_axis=0, concat_axis=0, tiled=True)
         operands = [bands] + [
             in_vmem(x) for x in (level, east, north, bathy, wet, east_open, north_open, synth, table)
@@ -493,16 +531,18 @@
         if last:
             own = jax.ShapeDtypeStruct((rows, cols), HIGH)
             return pl.pallas_call(
-                lambda *refs: grid_kernel(padded_rows, True, *refs),
+                lambda *refs: grid_kernel(padded_rows, True, True, *refs),
                 out_shape=(own,) * 3,
                 in_specs=[VMEM] * 9,
-                out_specs=(VMEM,) * 3,
-                scratch_shapes=scratch,
+                out_specs=(pl.BlockSpec(memory_space=pl.ANY),) * 3,
+                scratch_shapes=[pltpu.VMEM((rows, cols), HIGH)] * 3
+                + scratch
+                + [pltpu.SemaphoreType.DMA((3 * -(-rows // LEAVE),))],
                 compiler_params=small,
                 name="grid_last",
             )(*operands[:9])
         level, east, north, sums = pl.pallas_call(
-            lambda *refs: grid_kernel(padded_rows, False, *refs),
+            lambda *refs, near=STEPS - 1 - step < 8: grid_kernel(padded_rows, False, near, *refs),
             out_shape=(field, field, field, message),
             in_specs=[VMEM] * 10,
             out_specs=(VMEM,) * 4,

time: 480 us -> 477 us (level)
    all_to_all x1, waiting for transfers between devices: 8.06 us -> 1.65 us  [shards(): lax.all_to_all(sums, BOTH, split_axis=0, concat_axis=0, tiled=True)]
  transfers between devices with their start and end apart: 5 -> 5, of which waited for: 1 -> 2; matrix products, arithmetic and copies ran while one was open for 1% -> 0% of each run, Pallas kernels for 2% -> 3%
where the time goes in v5:
time: 477 us; the launch traced here: 469 us
  blocking collectives  346 us (73%)
  Pallas kernels  93.7 us (20%)
  starting transfers between devices  15.4 us (3%)
  local copies, waits for them, and re-layouts  5.92 us (1%)
    all_to_all x12, blocking collectives, shards(): bands = lax.all_to_all(back, BOTH, split_axis=0, concat_axis=0, tiled=True)  184 us
    all_to_all x11, blocking collectives, shards(): lax.all_to_all(sums, BOTH, split_axis=0, concat_axis=0, tiled=True)  162 us
    pallas_call x12, Pallas kernels, shards(): pl.pallas_call(lambda *refs: legendre_kernel(rows, *refs), out_shape=mess...  38.5 us
    pallas_call x11, Pallas kernels, shards(): pl.pallas_call(lambda *refs, near=STEPS - 1 - step < 8: grid_kernel(padde...  38.1 us
    all_to_all x1, starting transfers between devices, shards(): lax.all_to_all(sums, BOTH, split_axis=0, concat_axis=0, tiled=True)  11.5 us
  transfers between devices with their start and end apart: 5, of which 2 were waited for; matrix products, arithmetic and copies ran while one was open for 0% of the time, Pallas kernels for 3%

profile of v5, /device:TPU:1, one launch (start us, length us, event | category | flops | bytes accessed | tf_op | source)
XLA Modules:
  0.0 468.6 jit_solution(11141564287836803564)
XLA Ops:
  4.7 11.5 %all-to-all-start = ((f32[128,1,384]{2,1,0:T(1,128)}), f32[128,1,384]{2,1,0:T(1,128)S(1)}, u32[]{:S(2)}, u32[]{:S(2)}) async-start(f32[128,1,384]{2,1,0:T(1,128)} %copy.45), calls=%async_computation | async-start | bytes 393216 | tf_op jit(solution)/shard_map/all_to_all | solution.py:493
  37.4 22.6 %all_to_all.264 = f32[128,1,384]{2,1,0:T(1,128)S(1)} all-to-all(f32[128,1,384]{2,1,0:T(1,128)S(1)} %copy.46), channel_id=1, replica_groups=mesh['lat'=32,'lon'=4] {'lat','lon'}, dimensions={0} | all-to-all | bytes 393216 | tf_op jit(solution)/shard_map/all_to_all | solution.py:526
  66.7 14.6 %all_to_all.265 = f32[128,1,384]{2,1,0:T(1,128)S(1)} all-to-all(f32[128,1,384]{2,1,0:T(1,128)S(1)} %copy.47), channel_id=1, replica_groups=mesh['lat'=32,'lon'=4] {'lat','lon'}, dimensions={0} | all-to-all | bytes 393216 | tf_op jit(solution)/shard_map/all_to_all | solution.py:493
  84.7 14.6 %all_to_all.266 = f32[128,1,384]{2,1,0:T(1,128)S(1)} all-to-all(f32[128,1,384]{2,1,0:T(1,128)S(1)} %copy.48), channel_id=1, replica_groups=mesh['lat'=32,'lon'=4] {'lat','lon'}, dimensions={0} | all-to-all | bytes 393216 | tf_op jit(solution)/shard_map/all_to_all | solution.py:526
  103.1 14.6 %all_to_all.267 = f32[128,1,384]{2,1,0:T(1,128)S(1)} all-to-all(f32[128,1,384]{2,1,0:T(1,128)S(1)} %copy.49), channel_id=1, replica_groups=mesh['lat'=32,'lon'=4] {'lat','lon'}, dimensions={0} | all-to-all | bytes 393216 | tf_op jit(solution)/shard_map/all_to_all | solution.py:493
  121.1 14.6 %all_to_all.268 = f32[128,1,384]{2,1,0:T(1,128)S(1)} all-to-all(f32[128,1,384]{2,1,0:T(1,128)S(1)} %copy.50), channel_id=1, replica_groups=mesh['lat'=32,'lon'=4] {'lat','lon'}, dimensions={0} | all-to-all | bytes 393216 | tf_op jit(solution)/shard_map/all_to_all | solution.py:526
  139.4 14.6 %all_to_all.269 = f32[128,1,384]{2,1,0:T(1,128)S(1)} all-to-all(f32[128,1,384]{2,1,0:T(1,128)S(1)} %copy.51), channel_id=1, replica_groups=mesh['lat'=32,'lon'=4] {'lat','lon'}, dimensions={0} | all-to-all | bytes 393216 | tf_op jit(solution)/shard_map/all_to_all | solution.py:493
  157.5 14.8 %all_to_all.270 = f32[128,1,384]{2,1,0:T(1,128)S(1)} all-to-all(f32[128,1,384]{2,1,0:T(1,128)S(1)} %copy.52), channel_id=1, replica_groups=mesh['lat'=32,'lon'=4] {'lat','lon'}, dimensions={0} | all-to-all | bytes 393216 | tf_op jit(solution)/shard_map/all_to_all | solution.py:526
  176.1 14.6 %all_to_all.271 = f32[128,1,384]{2,1,0:T(1,128)S(1)} all-to-all(f32[128,1,384]{2,1,0:T(1,128)S(1)} %copy.53), channel_id=1, replica_groups=mesh['lat'=32,'lon'=4] {'lat','lon'}, dimensions={0} | all-to-all | bytes 393216 | tf_op jit(solution)/shard_map/all_to_all | solution.py:493
  194.2 14.6 %all_to_all.272 = f32[128,1,384]{2,1,0:T(1,128)S(1)} all-to-all(f32[128,1,384]{2,1,0:T(1,128)S(1)} %copy.54), channel_id=1, replica_groups=mesh['lat'=32,'lon'=4] {'lat','lon'}, dimensions={0} | all-to-all | bytes 393216 | tf_op jit(solution)/shard_map/all_to_all | solution.py:526
  212.4 14.9 %all_to_all.273 = f32[128,1,384]{2,1,0:T(1,128)S(1)} all-to-all(f32[128,1,384]{2,1,0:T(1,128)S(1)} %copy.55), channel_id=1, replica_groups=mesh['lat'=32,'lon'=4] {'lat','lon'}, dimensions={0} | all-to-all | bytes 393216 | tf_op jit(solution)/shard_map/all_to_all | solution.py:493
  230.8 14.6 %all_to_all.274 = f32[128,1,384]{2,1,0:T(1,128)S(1)} all-to-all(f32[128,1,384]{2,1,0:T(1,128)S(1)} %copy.56), channel_id=1, replica_groups=mesh['lat'=32,'lon'=4] {'lat','lon'}, dimensions={0} | all-to-all | bytes 393216 | tf_op jit(solution)/shard_map/all_to_all | solution.py:526
  249.1 14.6 %all_to_all.275 = f32[128,1,384]{2,1,0:T(1,128)S(1)} all-to-all(f32[128,1,384]{2,1,0:T(1,128)S(1)} %copy.57), channel_id=1, replica_groups=mesh['lat'=32,'lon'=4] {'lat','lon'}, dimensions={0} | all-to-all | bytes 393216 | tf_op jit(solution)/shard_map/all_to_all | solution.py:493
  267.1 15.1 %all_to_all.276 = f32[128,1,384]{2,1,0:T(1,128)S(1)} all-to-all(f32[128,1,384]{2,1,0:T(1,128)S(1)} %copy.58), channel_id=1, replica_groups=mesh['lat'=32,'lon'=4] {'lat','lon'}, dimensions={0} | all-to-all | bytes 393216 | tf_op jit(solution)/shard_map/all_to_all | solution.py:526
  285.8 14.6 %all_to_all.277 = f32[128,1,384]{2,1,0:T(1,128)S(1)} all-to-all(f32[128,1,384]{2,1,0:T(1,128)S(1)} %copy.59), channel_id=1, replica_groups=mesh['lat'=32,'lon'=4] {'lat','lon'}, dimensions={0} | all-to-all | bytes 393216 | tf_op jit(solution)/shard_map/all_to_all | solution.py:493
  303.9 14.6 %all_to_all.278 = f32[128,1,384]{2,1,0:T(1,128)S(1)} all-to-all(f32[128,1,384]{2,1,0:T(1,128)S(1)} %copy.60), channel_id=1, replica_groups=mesh['lat'=32,'lon'=4] {'lat','lon'}, dimensions={0} | all-to-all | bytes 393216 | tf_op jit(solution)/shard_map/all_to_all | solution.py:526
  322.2 14.8 %all_to_all.279 = f32[128,1,384]{2,1,0:T(1,128)S(1)} all-to-all(f32[128,1,384]{2,1,0:T(1,128)S(1)} %copy.61), channel_id=1, replica_groups=mesh['lat'=32,'lon'=4] {'lat','lon'}, dimensions={0} | all-to-all | bytes 393216 | tf_op jit(solution)/shard_map/all_to_all | solution.py:493
  340.5 14.6 %all_to_all.280 = f32[128,1,384]{2,1,0:T(1,128)S(1)} all-to-all(f32[128,1,384]{2,1,0:T(1,128)S(1)} %copy.62), channel_id=1, replica_groups=mesh['lat'=32,'lon'=4] {'lat','lon'}, dimensions={0} | all-to-all | bytes 393216 | tf_op jit(solution)/shard_map/all_to_all | solution.py:526
  358.8 14.6 %all_to_all.281 = f32[128,1,384]{2,1,0:T(1,128)S(1)} all-to-all(f32[128,1,384]{2,1,0:T(1,128)S(1)} %copy.63), channel_id=1, replica_groups=mesh['lat'=32,'lon'=4] {'lat','lon'}, dimensions={0} | all-to-all | bytes 393216 | tf_op jit(solution)/shard_map/all_to_all | solution.py:493
  376.8 14.9 %all_to_all.282 = f32[128,1,384]{2,1,0:T(1,128)S(1)} all-to-all(f32[128,1,384]{2,1,0:T(1,128)S(1)} %copy.64), channel_id=1, replica_groups=mesh['lat'=32,'lon'=4] {'lat','lon'}, dimensions={0} | all-to-all | bytes 393216 | tf_op jit(solution)/shard_map/all_to_all | solution.py:526
  395.4 14.6 %all_to_all.283 = f32[128,1,384]{2,1,0:T(1,128)S(1)} all-to-all(f32[128,1,384]{2,1,0:T(1,128)S(1)} %copy.65), channel_id=1, replica_groups=mesh['lat'=32,'lon'=4] {'lat','lon'}, dimensions={0} | all-to-all | bytes 393216 | tf_op jit(solution)/shard_map/all_to_all | solution.py:493
  413.4 14.6 %all_to_all.284 = f32[128,1,384]{2,1,0:T(1,128)S(1)} all-to-all(f32[128,1,384]{2,1,0:T(1,128)S(1)} %copy.66), channel_id=1, replica_groups=mesh['lat'=32,'lon'=4] {'lat','lon'}, dimensions={0} | all-to-all | bytes 393216 | tf_op jit(solution)/shard_map/all_to_all | solution.py:526
  431.7 14.9 %all_to_all.285 = f32[128,1,384]{2,1,0:T(1,128)S(1)} all-to-all(f32[128,1,384]{2,1,0:T(1,128)S(1)} %copy.67), channel_id=1, replica_groups=mesh['lat'=32,'lon'=4] {'lat','lon'}, dimensions={0} | all-to-all | bytes 393216 | tf_op jit(solution)/shard_map/all_to_all | solution.py:493
  450.1 14.6 %all_to_all.286 = f32[128,1,384]{2,1,0:T(1,128)S(1)} all-to-all(f32[128,1,384]{2,1,0:T(1,128)S(1)} %copy.68), channel_id=1, replica_groups=mesh['lat'=32,'lon'=4] {'lat','lon'}, dimensions={0} | all-to-all | bytes 393216 | tf_op jit(solution)/shard_map/all_to_all | solution.py:526
  (99 shorter events, 109.6 us)
Async XLA Ops:
  0.6 2.2 copy-start
  4.7 22.2 %all-to-all-start = ((f32[128,1,384]{2,1,0:T(1,128)}), f32[128,1,384]{2,1,0:T(1,128)S(1)}, u32[]{:S(2)}, u32[]{:S(2)}) async-start(f32[128,1,384]{2,1,0:T(1,128)} %copy.45), calls=%async_computation | async-start | bytes 393216 | tf_op jit(solution)/shard_map/all_to_all | solution.py:493
  17.6 4.1 collective-permute-start
  18.8 3.0 collective-permute-start.1
  23.9 36.1 %collective-permute-start.2 = (f32[64,2432]{1,0:T(8,128)}, f32[64,2432]{1,0:T(8,128)S(1)}, u32[]{:S(2)}, u32[]{:S(2)}) collective-permute-start(f32[64,2432]{1,0:T(8,128)} %row_edges.2), channel_id=1, source_target_pairs={{0,4},{8,12},{16,20},{24,28},{32,36},{40,44},{48,52},{56,60},{64,6... | collective-permute-start | bytes 1867784 | tf_op jit(solution)/shard_map/ppermute | solution.py:462
  26.9 2.2 copy-start.2
  27.0 2.2 copy-start.1
  28.4 31.6 %collective-permute-start.3 = (f32[64,2432]{1,0:T(8,128)S(1)}, f32[64,2432]{1,0:T(8,128)S(1)}, u32[]{:S(2)}, u32[]{:S(2)}) collective-permute-start(f32[64,2432]{1,0:T(8,128)S(1)} %row_edges.3), channel_id=1, source_target_pairs={{4,8},{12,16},{20,24},{28,32},{36,40},{44,48},{52,56},{60,64},{68,... | collective-permute-start | bytes 1867784 | tf_op jit(solution)/shard_map/ppermute | solution.py:462

commit v6 on v5

--- a/solution.py
+++ b/solution.py
@@ -66,7 +66,7 @@
         base, block = tile * every, slice(tile * LANES, (tile + 1) * LANES)
         for part in range(4):
             line_ref[pl.ds(base + part, every // 4, stride=4), :] = message[:, block]
-        out_ref[:, block] = line_ref[base : base + every, :]
+        out_ref[:, 0, block] = line_ref[base : base + every, :]
 
 
 def second_part(message):
@@ -300,7 +300,7 @@
     result = jnp.where(lanes_of(parts[0].shape) < SECOND, parts[0], parts[1])
     for index in range(bands):
         at = bands - 1 - index
-        out_ref[4 * index : 4 * index + 4, :] = jnp.broadcast_to(result[at : at + 1, :], (4, MSG))
+        out_ref[4 * index : 4 * index + 4, 0, :] = jnp.broadcast_to(result[at : at + 1, :], (4, MSG))
 
 
 def ghost_tile(index, east, west):
@@ -408,7 +408,7 @@
     legendre = legendre.reshape(legendre.shape[1:])
     degrees = legendre.shape[1]
     small = pltpu.CompilerParams(vmem_limit_bytes=12 * 2**20)
-    message = jax.ShapeDtypeStruct((devices, MSG), HIGH)
+    message = jax.ShapeDtypeStruct((devices, 1, MSG), HIGH)
     field = jax.ShapeDtypeStruct((tall, wide), HIGH)
     line = pltpu.VMEM((MSG // LANES * devices, LANES), HIGH)
     fields = [height, flux_east, flux_north, bathymetry, wet_mask]
@@ -490,7 +490,7 @@
     tiles = pltpu.VMEM((80, LANES), HIGH)
     for step in range(STEPS):
         first, last = step == 0, step == STEPS - 1
-        spectral = lax.all_to_all(sums, BOTH, split_axis=0, concat_axis=0, tiled=True)
+        spectral = lax.all_to_all(sums, BOTH, split_axis=0, concat_axis=0, tiled=True)[:, 0]
         if first:
             late = swapped(row_edge(1 - even, spectral), 1)
             legendre, turned = pl.pallas_call(
@@ -523,7 +523,7 @@
                 compiler_params=small,
                 name="assemble",
             )(*[in_hbm(f) for f in fields], from_east, from_west, early, late, even)
-        bands = lax.all_to_all(back, BOTH, split_axis=0, concat_axis=0, tiled=True)
+        bands = lax.all_to_all(back, BOTH, split_axis=0, concat_axis=0, tiled=True)[:, 0]
         operands = [bands] + [
             in_vmem(x) for x in (level, east, north, bathy, wet, east_open, north_open, synth, table)
         ]

time: 477 us -> 473 us (level)
  local copies, waits for them, and re-layouts: 5.92 us -> 0.36 us
    all_to_all x24 -> x0, local copies, waits for them, and re-layouts: 5.56 us -> none  [the longest x12 3.12 us: shards(): lax.all_to_all(sums, BOTH, split_axis=0, concat_axis=0, tiled=True)]
where the time goes in v6:
time: 473 us; the launch traced here: 465 us
  blocking collectives  346 us (73%)
  Pallas kernels  95.5 us (20%)
  starting transfers between devices  15.4 us (3%)
    all_to_all x12, blocking collectives, shards(): lax.all_to_all(back, BOTH, split_axis=0, concat_axis=0, tiled=True)[:, 0]  184 us
    all_to_all x11, blocking collectives, shards(): lax.all_to_all(sums, BOTH, split_axis=0, concat_axis=0, tiled=True)[:, 0]  162 us
    pallas_call x11, Pallas kernels, shards(): pl.pallas_call(lambda *refs, near=STEPS - 1 - step < 8: grid_kernel(padde...  39.1 us
    pallas_call x12, Pallas kernels, shards(): pl.pallas_call(lambda *refs: legendre_kernel(rows, *refs), out_shape=mess...  38.6 us
    all_to_all x1, starting transfers between devices, shards(): lax.all_to_all(sums, BOTH, split_axis=0, concat_axis=0, tiled=True)[:, 0]  11.5 us
  transfers between devices with their start and end apart: 5, of which 2 were waited for; matrix products, arithmetic and copies ran while one was open for 0% of the time, Pallas kernels for 3%

profile of v6, /device:TPU:1, one launch (start us, length us, event | category | flops | bytes accessed | tf_op | source)
XLA Modules:
  0.0 464.7 jit_solution(396783015974411133)
XLA Ops:
  4.5 11.5 %all-to-all-start = ((f32[128,1,384]{2,1,0:T(1,128)}), f32[128,1,384]{2,1,0:T(1,128)S(1)}, u32[]{:S(2)}, u32[]{:S(2)}) async-start(f32[128,1,384]{2,1,0:T(1,128)} %get-tuple-element.61.refs_14_), calls=%async_computation | async-start | bytes 393216 | tf_op jit(solution)/shard_map/all_to_all | solution.py:493
  37.0 22.6 %all_to_all.120 = f32[128,1,384]{2,1,0:T(1,128)S(1)} all-to-all(f32[128,1,384]{2,1,0:T(1,128)S(1)} %legendre_pair.12), channel_id=1, replica_groups=mesh['lat'=32,'lon'=4] {'lat','lon'}, dimensions={0} | all-to-all | bytes 393216 | tf_op jit(solution)/shard_map/all_to_all | solution.py:526
  66.2 14.6 %all_to_all.121 = f32[128,1,384]{2,1,0:T(1,128)S(1)} all-to-all(f32[128,1,384]{2,1,0:T(1,128)S(1)} %get-tuple-element.75), channel_id=1, replica_groups=mesh['lat'=32,'lon'=4] {'lat','lon'}, dimensions={0} | all-to-all | bytes 393216 | tf_op jit(solution)/shard_map/all_to_all | solution.py:493
  84.1 14.6 %all_to_all.122 = f32[128,1,384]{2,1,0:T(1,128)S(1)} all-to-all(f32[128,1,384]{2,1,0:T(1,128)S(1)} %legendre_pair.13), channel_id=1, replica_groups=mesh['lat'=32,'lon'=4] {'lat','lon'}, dimensions={0} | all-to-all | bytes 393216 | tf_op jit(solution)/shard_map/all_to_all | solution.py:526
  102.3 14.6 %all_to_all.123 = f32[128,1,384]{2,1,0:T(1,128)S(1)} all-to-all(f32[128,1,384]{2,1,0:T(1,128)S(1)} %get-tuple-element.79), channel_id=1, replica_groups=mesh['lat'=32,'lon'=4] {'lat','lon'}, dimensions={0} | all-to-all | bytes 393216 | tf_op jit(solution)/shard_map/all_to_all | solution.py:493
  120.1 14.6 %all_to_all.124 = f32[128,1,384]{2,1,0:T(1,128)S(1)} all-to-all(f32[128,1,384]{2,1,0:T(1,128)S(1)} %legendre_pair.14), channel_id=1, replica_groups=mesh['lat'=32,'lon'=4] {'lat','lon'}, dimensions={0} | all-to-all | bytes 393216 | tf_op jit(solution)/shard_map/all_to_all | solution.py:526
  138.4 14.6 %all_to_all.125 = f32[128,1,384]{2,1,0:T(1,128)S(1)} all-to-all(f32[128,1,384]{2,1,0:T(1,128)S(1)} %get-tuple-element.83), channel_id=1, replica_groups=mesh['lat'=32,'lon'=4] {'lat','lon'}, dimensions={0} | all-to-all | bytes 393216 | tf_op jit(solution)/shard_map/all_to_all | solution.py:493
  156.2 14.8 %all_to_all.126 = f32[128,1,384]{2,1,0:T(1,128)S(1)} all-to-all(f32[128,1,384]{2,1,0:T(1,128)S(1)} %legendre_pair.15), channel_id=1, replica_groups=mesh['lat'=32,'lon'=4] {'lat','lon'}, dimensions={0} | all-to-all | bytes 393216 | tf_op jit(solution)/shard_map/all_to_all | solution.py:526
  174.7 14.6 %all_to_all.127 = f32[128,1,384]{2,1,0:T(1,128)S(1)} all-to-all(f32[128,1,384]{2,1,0:T(1,128)S(1)} %get-tuple-element.87), channel_id=1, replica_groups=mesh['lat'=32,'lon'=4] {'lat','lon'}, dimensions={0} | all-to-all | bytes 393216 | tf_op jit(solution)/shard_map/all_to_all | solution.py:493
  192.6 14.6 %all_to_all.128 = f32[128,1,384]{2,1,0:T(1,128)S(1)} all-to-all(f32[128,1,384]{2,1,0:T(1,128)S(1)} %legendre_pair.16), channel_id=1, replica_groups=mesh['lat'=32,'lon'=4] {'lat','lon'}, dimensions={0} | all-to-all | bytes 393216 | tf_op jit(solution)/shard_map/all_to_all | solution.py:526
  210.7 14.9 %all_to_all.129 = f32[128,1,384]{2,1,0:T(1,128)S(1)} all-to-all(f32[128,1,384]{2,1,0:T(1,128)S(1)} %get-tuple-element.91), channel_id=1, replica_groups=mesh['lat'=32,'lon'=4] {'lat','lon'}, dimensions={0} | all-to-all | bytes 393216 | tf_op jit(solution)/shard_map/all_to_all | solution.py:493
  228.8 14.6 %all_to_all.130 = f32[128,1,384]{2,1,0:T(1,128)S(1)} all-to-all(f32[128,1,384]{2,1,0:T(1,128)S(1)} %legendre_pair.17), channel_id=1, replica_groups=mesh['lat'=32,'lon'=4] {'lat','lon'}, dimensions={0} | all-to-all | bytes 393216 | tf_op jit(solution)/shard_map/all_to_all | solution.py:526
  247.0 14.6 %all_to_all.131 = f32[128,1,384]{2,1,0:T(1,128)S(1)} all-to-all(f32[128,1,384]{2,1,0:T(1,128)S(1)} %get-tuple-element.95), channel_id=1, replica_groups=mesh['lat'=32,'lon'=4] {'lat','lon'}, dimensions={0} | all-to-all | bytes 393216 | tf_op jit(solution)/shard_map/all_to_all | solution.py:493
  264.8 15.1 %all_to_all.132 = f32[128,1,384]{2,1,0:T(1,128)S(1)} all-to-all(f32[128,1,384]{2,1,0:T(1,128)S(1)} %legendre_pair.18), channel_id=1, replica_groups=mesh['lat'=32,'lon'=4] {'lat','lon'}, dimensions={0} | all-to-all | bytes 393216 | tf_op jit(solution)/shard_map/all_to_all | solution.py:526
  283.5 14.6 %all_to_all.133 = f32[128,1,384]{2,1,0:T(1,128)S(1)} all-to-all(f32[128,1,384]{2,1,0:T(1,128)S(1)} %get-tuple-element.99), channel_id=1, replica_groups=mesh['lat'=32,'lon'=4] {'lat','lon'}, dimensions={0} | all-to-all | bytes 393216 | tf_op jit(solution)/shard_map/all_to_all | solution.py:493
  301.3 14.6 %all_to_all.134 = f32[128,1,384]{2,1,0:T(1,128)S(1)} all-to-all(f32[128,1,384]{2,1,0:T(1,128)S(1)} %legendre_pair.19), channel_id=1, replica_groups=mesh['lat'=32,'lon'=4] {'lat','lon'}, dimensions={0} | all-to-all | bytes 393216 | tf_op jit(solution)/shard_map/all_to_all | solution.py:526
  319.4 14.9 %all_to_all.135 = f32[128,1,384]{2,1,0:T(1,128)S(1)} all-to-all(f32[128,1,384]{2,1,0:T(1,128)S(1)} %get-tuple-element.103), channel_id=1, replica_groups=mesh['lat'=32,'lon'=4] {'lat','lon'}, dimensions={0} | all-to-all | bytes 393216 | tf_op jit(solution)/shard_map/all_to_all | solution.py:493
  337.5 14.6 %all_to_all.136 = f32[128,1,384]{2,1,0:T(1,128)S(1)} all-to-all(f32[128,1,384]{2,1,0:T(1,128)S(1)} %legendre_pair.20), channel_id=1, replica_groups=mesh['lat'=32,'lon'=4] {'lat','lon'}, dimensions={0} | all-to-all | bytes 393216 | tf_op jit(solution)/shard_map/all_to_all | solution.py:526
  355.7 14.6 %all_to_all.137 = f32[128,1,384]{2,1,0:T(1,128)S(1)} all-to-all(f32[128,1,384]{2,1,0:T(1,128)S(1)} %get-tuple-element.107), channel_id=1, replica_groups=mesh['lat'=32,'lon'=4] {'lat','lon'}, dimensions={0} | all-to-all | bytes 393216 | tf_op jit(solution)/shard_map/all_to_all | solution.py:493
  373.5 14.9 %all_to_all.138 = f32[128,1,384]{2,1,0:T(1,128)S(1)} all-to-all(f32[128,1,384]{2,1,0:T(1,128)S(1)} %legendre_pair.21), channel_id=1, replica_groups=mesh['lat'=32,'lon'=4] {'lat','lon'}, dimensions={0} | all-to-all | bytes 393216 | tf_op jit(solution)/shard_map/all_to_all | solution.py:526
  392.0 14.6 %all_to_all.139 = f32[128,1,384]{2,1,0:T(1,128)S(1)} all-to-all(f32[128,1,384]{2,1,0:T(1,128)S(1)} %get-tuple-element.111), channel_id=1, replica_groups=mesh['lat'=32,'lon'=4] {'lat','lon'}, dimensions={0} | all-to-all | bytes 393216 | tf_op jit(solution)/shard_map/all_to_all | solution.py:493
  409.8 14.6 %all_to_all.140 = f32[128,1,384]{2,1,0:T(1,128)S(1)} all-to-all(f32[128,1,384]{2,1,0:T(1,128)S(1)} %legendre_pair.22), channel_id=1, replica_groups=mesh['lat'=32,'lon'=4] {'lat','lon'}, dimensions={0} | all-to-all | bytes 393216 | tf_op jit(solution)/shard_map/all_to_all | solution.py:526
  428.0 14.9 %all_to_all.141 = f32[128,1,384]{2,1,0:T(1,128)S(1)} all-to-all(f32[128,1,384]{2,1,0:T(1,128)S(1)} %get-tuple-element.115), channel_id=1, replica_groups=mesh['lat'=32,'lon'=4] {'lat','lon'}, dimensions={0} | all-to-all | bytes 393216 | tf_op jit(solution)/shard_map/all_to_all | solution.py:493
  446.1 14.6 %all_to_all.142 = f32[128,1,384]{2,1,0:T(1,128)S(1)} all-to-all(f32[128,1,384]{2,1,0:T(1,128)S(1)} %legendre_pair.23), channel_id=1, replica_groups=mesh['lat'=32,'lon'=4] {'lat','lon'}, dimensions={0} | all-to-all | bytes 393216 | tf_op jit(solution)/shard_map/all_to_all | solution.py:526
  (75 shorter events, 105.9 us)
Async XLA Ops:
  0.6 2.2 copy-start
  4.5 22.2 %all-to-all-start = ((f32[128,1,384]{2,1,0:T(1,128)}), f32[128,1,384]{2,1,0:T(1,128)S(1)}, u32[]{:S(2)}, u32[]{:S(2)}) async-start(f32[128,1,384]{2,1,0:T(1,128)} %get-tuple-element.61.refs_14_), calls=%async_computation | async-start | bytes 393216 | tf_op jit(solution)/shard_map/all_to_all | solution.py:493
  17.5 4.1 collective-permute-start
  18.6 3.0 collective-permute-start.1
  23.7 35.9 %collective-permute-start.2 = (f32[64,2432]{1,0:T(8,128)}, f32[64,2432]{1,0:T(8,128)S(1)}, u32[]{:S(2)}, u32[]{:S(2)}) collective-permute-start(f32[64,2432]{1,0:T(8,128)} %row_edges.2), channel_id=1, source_target_pairs={{0,4},{8,12},{16,20},{24,28},{32,36},{40,44},{48,52},{56,60},{64,6... | collective-permute-start | bytes 1867784 | tf_op jit(solution)/shard_map/ppermute | solution.py:462
  26.8 2.2 copy-start.2
  26.8 2.2 copy-start.1
  28.3 31.4 %collective-permute-start.3 = (f32[64,2432]{1,0:T(8,128)S(1)}, f32[64,2432]{1,0:T(8,128)S(1)}, u32[]{:S(2)}, u32[]{:S(2)}) collective-permute-start(f32[64,2432]{1,0:T(8,128)S(1)} %row_edges.3), channel_id=1, source_target_pairs={{4,8},{12,16},{20,24},{28,32},{36,40},{44,48},{52,56},{60,64},{68,... | collective-permute-start | bytes 1867784 | tf_op jit(solution)/shard_map/ppermute | solution.py:462
